TPU v7x, 32 devices: a whole 2x2x4 slice. The times are simulated.
32 devices in a mesh: groups: 2 (over y), tensor: 16 (over z, x, core).
Axes of the slice: x: 2, y: 2, z: 4, core: 2. Of those that a mesh axis runs over, the one named last changes fastest.
Arguments:
- activations: bfloat16 [64, 16384], P('groups', 'tensor'), parts along dimension 0
- signs: int32 [16384], P('tensor'), may hold values from -1 to 1, as said below
Outputs:
- hessian: float32 [32768, 16384], P(('groups', 'tensor')), parts along dimension 0
There are 2 independent parts, one for each index of `groups`. A program takes and returns all parts, laid end to end along the dimension named above; an argument that names none is the same for every part. Nothing has to cross between parts.
Inputs may be any that keep to these rules, and one draw needn't show every extreme that they name: `signs`: each entry is -1 or +1.
All inputs are finite; a program needn't handle non-finite values.
Results may differ from a plain program's by a relative error of at most 0.0057.
Values may be sent and summed in bfloat16 or wider, within the bound.
No kernel may reach another device: no remote copies, remote signals or barrier semaphores. Data moves between devices by JAX's collectives and lax.ppermute only.
A program may use at most 384 MiB of HBM per device.

v0:
```python
import jax
import jax.numpy as jnp
from jax import lax
from jax.sharding import PartitionSpec as P

D = 16384
INNER_ORDER = 128
OUTER_ORDER = 128


def hadamard_matrix(order):
    first = jnp.arange(order, dtype=jnp.int32)[:, None]
    second = jnp.arange(order, dtype=jnp.int32)[None, :]
    count = jnp.zeros((order, order), jnp.int32)
    for level in range(max(order.bit_length() - 1, 0)):
        count = count + jnp.right_shift(first, level) % 2 * (jnp.right_shift(second, level) % 2)
    return jnp.where(count % 2 == 0, 1.0, -1.0).astype(jnp.float32)


def per_device(activations, signs):
    token_batch, columns = activations.shape
    sign_flipped = activations * signs.astype(jnp.bfloat16)[None, :]
    inner_rot = jnp.dot(
        sign_flipped.reshape(token_batch * columns // INNER_ORDER, INNER_ORDER),
        hadamard_matrix(INNER_ORDER).astype(jnp.bfloat16),
        preferred_element_type=jnp.float32,
    )
    inner_rot = (
        (inner_rot / jnp.sqrt(jnp.float32(INNER_ORDER)))
        .reshape(token_batch, columns)
        .astype(jnp.bfloat16)
    )
    regrouped = lax.all_to_all(inner_rot, "tensor", split_axis=0, concat_axis=1, tiled=True)
    local_tokens = regrouped.shape[0]
    outer_rot = jnp.einsum(
        "tab,ae->teb",
        regrouped.reshape(local_tokens, OUTER_ORDER, INNER_ORDER),
        hadamard_matrix(OUTER_ORDER).astype(jnp.bfloat16),
        preferred_element_type=jnp.float32,
    )
    rotated_input = (
        (outer_rot / jnp.sqrt(jnp.float32(OUTER_ORDER)))
        .reshape(local_tokens, D)
        .astype(jnp.bfloat16)
    )
    ranks = lax.axis_size("tensor")
    row_groups = ranks // 16
    sub_rows = columns // row_groups
    tile_rows = D // row_groups
    tile_cols = D // 16
    row_parts = (
        rotated_input.reshape(local_tokens, ranks, row_groups, sub_rows)
        .transpose(2, 0, 1, 3)
        .reshape(row_groups, local_tokens, tile_rows)
    )
    col_parts = rotated_input.reshape(local_tokens, 16, tile_cols).transpose(1, 0, 2)
    row_wide = jnp.broadcast_to(row_parts[:, None], (row_groups, 16, local_tokens, tile_rows))
    col_wide = jnp.broadcast_to(col_parts[None], (row_groups, 16, local_tokens, tile_cols))
    outgoing = jnp.concatenate([row_wide, col_wide], axis=3).reshape(
        ranks, local_tokens, tile_rows + tile_cols
    )
    arriving_rows = lax.all_to_all(outgoing, "tensor", split_axis=0, concat_axis=1, tiled=True)[0]
    tile_gram = lax.dot_general(
        arriving_rows[:, :tile_rows],
        arriving_rows[:, tile_rows:],
        (((0,), (0,)), ((), ())),
        preferred_element_type=jnp.float32,
    )
    returned = lax.all_to_all(
        tile_gram.reshape(ranks, sub_rows, tile_cols),
        "tensor",
        split_axis=0,
        concat_axis=0,
        tiled=True,
    )
    gram_rows = (
        returned.reshape(row_groups, 16, sub_rows, tile_cols)
        .transpose(0, 2, 1, 3)
        .reshape(columns, D)
    )
    return gram_rows / jnp.float32(token_batch)


def solution(mesh):
    return jax.shard_map(
        per_device,
        mesh=mesh,
        in_specs=(P("groups", "tensor"), P("tensor")),
        out_specs=P(("groups", "tensor"), None),
        check_vma=False,
    )
```

profile of v0, /device:TPU:0, one launch (start us, length us, event | category | flops | bytes accessed | tf_op | source)
XLA Modules:
  0.0 1615.0 jit_solution(13894933811081534172)
XLA Ops:
  0.0 0.7 convert_element_type.35
  0.7 0.8 broadcast_multiply_fusion
  1.6 0.3 fusion
  2.0 14.1 all_to_all.27
  16.1 0.3 fusion.1
  16.5 0.1 copy.4
  16.5 0.1 copy.10
  16.6 0.8 broadcast_in_dim.25
  17.4 1.0 maximum_bitcast_fusion
  18.4 31.1 %all_to_all.28 = bf16[16,2,17408]{2,1,0:T(2,128)(2,1)S(1)} all-to-all(bf16[16,2,17408]{2,1,0:T(2,128)(2,1)S(1)} %maximum_bitcast_fusion), channel_id=1, replica_groups=mesh['groups'=2,'tensor'=16] {'tensor'}, dimensions={0} | all-to-all | bytes 2228224 | tf_op jit(solution)/shard_map/all_to_all | solution.py:62
  49.5 0.4 squeeze.3
  50.0 25.2 %fusion.2 = f32[16384,1024]{1,0:T(8,128)} fusion(bf16[32,17408]{1,0:T(8,128)(2,1)S(1)} %squeeze.3), kind=kOutput, calls=%fused_computation.6 | convolution fusion | flops 1073741824 | bytes 68222976 | tf_op jit(solution)/shard_map/dot_general | solution.py:63
  75.2 1451.9 %all_to_all.29 = f32[16,1024,1024]{2,1,0:T(8,128)} all-to-all(f32[16,1024,1024]{2,1,0:T(8,128)} %bitcast.6), channel_id=1, replica_groups=mesh['groups'=2,'tensor'=16] {'tensor'}, dimensions={0} | all-to-all | bytes 134217728 | tf_op jit(solution)/shard_map/all_to_all | solution.py:69
  1527.1 44.2 %fusion.25 = f32[128,8,16,1024]{3,1,0,2:T(8,128)} fusion(f32[16,1024,1024]{2,1,0:T(8,128)} %all_to_all.29), kind=kLoop, calls=%fused_computation.56 | loop fusion | flops 16777216 | bytes 134217728
  1571.3 43.8 %copy.7 = f32[128,8,16,1024]{3,1,2,0:T(8,128)} copy(f32[128,8,16,1024]{3,1,0,2:T(8,128)} %fusion.25) | data formatting | bytes 134217728
  (9 shorter events, 0.2 us)
where the time goes:
time: 1620 us
  blocking collectives  1500 us (93%)
  other arithmetic  46.8 us (3%)
  local copies, waits for them, and re-layouts  45.3 us (3%)
  matrix products  25.9 us (2%)
    all_to_all x1, blocking collectives, per_device(): lax.all_to_all(tile_gram.reshape(ranks, sub_rows, tile_cols), 'tensor', s...  1450 us
    unnamed x1, other arithmetic  44.2 us
    unnamed x2, local copies, waits for them, and re-layouts  43.8 us

commit v1 on v0

v1 whole, which is shorter than its diff:
```python
import functools

import jax
import jax.numpy as jnp
from jax import lax
from jax.experimental import pallas as pl
from jax.experimental.pallas import tpu as pltpu
from jax.sharding import PartitionSpec as P

LANES = 128
CHUNK = 512
BUFFERS = 4


def butterfly(terms):
    step = 1
    while step < len(terms):
        out = list(terms)
        for low in range(len(terms)):
            if not low & step:
                out[low] = terms[low] + terms[low | step]
                out[low | step] = terms[low] - terms[low | step]
        terms = out
        step *= 2
    return terms


def odd_bits(value, order):
    shift = 1
    while shift < order.bit_length():
        shift *= 2
    while shift:
        value = value ^ (value >> shift)
        shift //= 2
    return value & 1


def hessian_kernel(ranks, mine_ref, other_ref, out_ref, wide, rotated, own_rows, tiles, sems):
    me = lax.axis_index("tensor")
    half, tokens, columns = mine_ref.shape
    local = columns // LANES
    width = ranks * columns

    row = lax.broadcasted_iota(jnp.int32, (LANES, LANES), 0)
    col = lax.broadcasted_iota(jnp.int32, (LANES, LANES), 1)
    inner = ((1 - 2 * odd_bits(row & col, LANES)).astype(jnp.float32) * (1.0 / LANES)).astype(jnp.bfloat16)
    for offset, ref in ((0, mine_ref), (1, other_ref)):

        @pl.loop(0, half)
        def _(k):
            block = ref[k]
            stacked = jnp.concatenate([block[:, j * LANES : (j + 1) * LANES] for j in range(local)], axis=0)
            spread = jnp.dot(stacked, inner, preferred_element_type=jnp.float32)
            terms = butterfly([spread[j * tokens : (j + 1) * tokens] for j in range(local)])
            for j in range(local):
                wide[2 * k + offset, j] = terms[j]

    signs = [(1 - 2 * odd_bits(me & m, ranks)).astype(jnp.float32) for m in range(ranks)]

    @pl.loop(0, local)
    def _(j):
        @pl.loop(0, tokens // 16)
        def _(t):
            rows = pl.ds(pl.multiple_of(t * 16, 16), 16)
            terms = butterfly([wide[k, j, rows, :] for k in range(ranks)])
            for m in range(ranks):
                at = pl.ds(pl.multiple_of((m * local + j) * LANES, LANES), LANES)
                rotated[rows, at] = (terms[m] * signs[m]).astype(jnp.bfloat16)

    own_rows[...] = rotated[:, pl.ds(pl.multiple_of(me * columns, LANES), columns)].T

    def copy(step, slot):
        at = pl.ds(pl.multiple_of(step * CHUNK, CHUNK), CHUNK)
        return pltpu.make_async_copy(tiles.at[slot], out_ref.at[:, at], sems.at[slot])

    @pl.loop(0, width // CHUNK // BUFFERS)
    def _(turn):
        for slot in range(BUFFERS):
            step = turn * BUFFERS + slot

            @pl.when(turn > 0)
            def _():
                copy(step - BUFFERS, slot).wait()

            at = pl.ds(pl.multiple_of(step * CHUNK, CHUNK), CHUNK)
            tiles[slot] = jnp.dot(own_rows[...], rotated[:, at], preferred_element_type=jnp.float32) * (1.0 / tokens)
            copy(step, slot).start()

    for slot in range(BUFFERS):
        copy(width // CHUNK - BUFFERS + slot, slot).wait()


def hessian_rows(ranks, mine, other):
    half, tokens, columns = mine.shape
    width = ranks * columns
    return pl.pallas_call(
        functools.partial(hessian_kernel, ranks),
        in_specs=[pl.BlockSpec(memory_space=pltpu.VMEM)] * 2,
        out_specs=pl.BlockSpec(memory_space=pl.ANY),
        out_shape=jax.ShapeDtypeStruct((columns, width), jnp.float32),
        scratch_shapes=[
            pltpu.VMEM((ranks, columns // LANES, tokens, LANES), jnp.float32),
            pltpu.VMEM((tokens, width), jnp.bfloat16),
            pltpu.VMEM((columns, tokens), jnp.bfloat16),
            pltpu.VMEM((BUFFERS, columns, CHUNK), jnp.float32),
            pltpu.SemaphoreType.DMA((BUFFERS,)),
        ],
        compiler_params=pltpu.CompilerParams(vmem_limit_bytes=40 * 2**20),
        cost_estimate=pl.CostEstimate(
            flops=2 * tokens * columns * width, bytes_accessed=4 * columns * width, transcendentals=0
        ),
    )(mine, other)


def per_device(ranks, activations, signs):
    flipped = activations * signs.astype(jnp.bfloat16)[None, :]

    def from_partner(x, k):
        return lax.ppermute(x, "tensor", [(i, i ^ k) for i in range(ranks)])

    far = range(4, ranks, 4)
    blocks = {0: flipped}
    for k in far:
        blocks[k] = from_partner(flipped, k)
    blocks[2] = from_partner(flipped, 2)
    crossed = from_partner(jnp.stack([blocks[k] for k in far]), 2)
    for i, k in enumerate(far):
        blocks[k + 2] = crossed[i]
    mine = jnp.stack([blocks[k] for k in range(0, ranks, 2)])
    return hessian_rows(ranks, mine, from_partner(mine, 1))


def solution(mesh):
    return jax.shard_map(
        functools.partial(per_device, mesh.shape["tensor"]),
        mesh=mesh,
        in_specs=(P("groups", "tensor"), P("tensor")),
        out_specs=P(("groups", "tensor"), None),
        check_vma=False,
    )
```

time: 1620 us -> 46.1 us (0.03)
  blocking collectives: 1500 us -> 0 us
  local copies, waits for them, and re-layouts: 45.3 us -> 0.04 us
  other arithmetic: 46.8 us -> 1.57 us
  matrix products: 25.9 us -> 0 us
  Pallas kernels: 0 us -> 24.8 us
    all_to_all x3 -> x0, blocking collectives: 1500 us -> none  [the longest x1 1450 us: per_device(): lax.all_to_all(tile_gram.reshape(ranks, sub_rows, tile_cols), 'tensor', s...]
    unnamed x2 -> x6, local copies, waits for them, and re-layouts: 43.8 us -> 0.04 us
    unnamed x1, other arithmetic: 44.2 us -> 0.86 us
    dot_general x3 -> x0, matrix products: 25.9 us -> none  [the longest x1 25.2 us: per_device(): lax.dot_general(arriving_rows[:, :tile_rows], arriving_rows[:, tile_rows:...]
    pallas_call x0 -> x1, Pallas kernels: none -> 24.8 us  [hessian_rows(): pl.pallas_call(functools.partial(hessian_kernel, ranks), in_specs=[pl.Blo...]
  transfers between devices with their start and end apart: 0 -> 6, of which waited for: 0 -> 4; matrix products, arithmetic and copies ran while one was open for 0% -> 0% of each run, Pallas kernels for 0% -> 0%
where the time goes in v1:
time: 46.1 us; the launch traced here: 45.9 us
  Pallas kernels  24.8 us (54%)
  waiting for transfers between devices  10.4 us (23%)
  starting transfers between devices  9.02 us (20%)
  other arithmetic  1.57 us (3%)
    pallas_call x1, Pallas kernels, hessian_rows(): pl.pallas_call(functools.partial(hessian_kernel, ranks), in_specs=[pl.Blo...  24.8 us
    ppermute x6, waiting for transfers between devices, from_partner(): return lax.ppermute(x, 'tensor', [(i, i ^ k) for i in range(ranks)])  10.4 us
    ppermute x6, starting transfers between devices, from_partner(): return lax.ppermute(x, 'tensor', [(i, i ^ k) for i in range(ranks)])  9.02 us
  transfers between devices with their start and end apart: 6, of which 4 were waited for; matrix products, arithmetic and copies ran while one was open for 0% of the time, Pallas kernels for 0%

profile of v1, /device:TPU:0, one launch (start us, length us, event | category | flops | bytes accessed | tf_op | source)
XLA Modules:
  0.0 45.9 jit_solution(8116068855327590313)
XLA Ops:
  0.0 0.7 %convert_element_type.3 = bf16[1024]{0:T(1024)(128)(2,1)S(1)} convert(s32[1024]{0:T(1024)} %param.3) | non-fusion elementwise | flops 1024 | bytes 6144 | tf_op jit(solution)/shard_map/convert_element_type | solution.py:116
  0.7 0.9 %bitcast_dynamic-update-slice_fusion.1 = (bf16[8,32,1024]{2,1,0:T(8,128)(2,1)S(1)}, bf16[32,1024]{1,0:T(8,128)(2,1)S(1)}) fusion(bf16[32,1024]{1,0:T(8,128)(2,1)} %param.2, bf16[1024]{0:T(1024)(128)(2,1)S(1)} %convert_element_type.3), kind=kLoop, calls=%fused_computation.5 | loop fusion | flops 131071 | bytes 198656
  1.5 4.1 %collective-permute-start.2 = (bf16[32,1024]{1,0:T(8,128)(2,1)S(1)}, bf16[32,1024]{1,0:T(8,128)(2,1)S(1)}, u32[]{:S(2)}, u32[]{:S(2)}) collective-permute-start(bf16[32,1024]{1,0:T(8,128)(2,1)S(1)} %get-tuple-element.6), channel_id=1, source_target_pairs={{0,8},{1,9},{2,10},{3,11},{4,12},{5,13},{6,14},{7,15},{8,0},{9,1},... | collective-permute-start | bytes 196616 | tf_op jit(solution)/shard_map/ppermute | solution.py:119
  5.7 1.6 %collective-permute-start.1 = (bf16[32,1024]{1,0:T(8,128)(2,1)S(1)}, bf16[32,1024]{1,0:T(8,128)(2,1)S(1)}, u32[]{:S(2)}, u32[]{:S(2)}) collective-permute-start(bf16[32,1024]{1,0:T(8,128)(2,1)S(1)} %get-tuple-element.6), channel_id=1, source_target_pairs={{0,4},{1,5},{2,6},{3,7},{4,0},{5,1},{6,2},{7,3},{8,12},{9,13},{10,... | collective-permute-start | bytes 196616 | tf_op jit(solution)/shard_map/ppermute | solution.py:119
  7.2 0.0 collective-permute-start.3
  7.2 1.7 %collective-permute-start = (bf16[32,1024]{1,0:T(8,128)(2,1)S(1)}, bf16[32,1024]{1,0:T(8,128)(2,1)S(1)}, u32[]{:S(2)}, u32[]{:S(2)}) collective-permute-start(bf16[32,1024]{1,0:T(8,128)(2,1)S(1)} %get-tuple-element.6), channel_id=1, source_target_pairs={{0,2},{1,3},{2,0},{3,1},{4,6},{5,7},{6,4},{7,5},{8,10},{9,11},{10,... | collective-permute-start | bytes 196616 | tf_op jit(solution)/shard_map/ppermute | solution.py:119
  8.9 0.0 collective-permute-done.2
  8.9 1.0 %collective-permute-done.1 = bf16[32,1024]{1,0:T(8,128)(2,1)S(1)} collective-permute-done((bf16[32,1024]{1,0:T(8,128)(2,1)S(1)}, bf16[32,1024]{1,0:T(8,128)(2,1)S(1)}, u32[]{:S(2)}, u32[]{:S(2)}) %collective-permute-start.1) | collective-permute-done | bytes 65568 | tf_op jit(solution)/shard_map/ppermute | solution.py:119
  9.9 3.4 %collective-permute-done.3 = bf16[32,1024]{1,0:T(8,128)(2,1)S(1)} collective-permute-done((bf16[32,1024]{1,0:T(8,128)(2,1)S(1)}, bf16[32,1024]{1,0:T(8,128)(2,1)S(1)}, u32[]{:S(2)}, u32[]{:S(2)}) %collective-permute-start.3) | collective-permute-done | bytes 65568 | tf_op jit(solution)/shard_map/ppermute | solution.py:119
  13.3 1.6 %collective-permute-start.4 = (bf16[3,32,1024]{2,1,0:T(8,128)(2,1)S(1)}, bf16[3,32,1024]{2,1,0:T(8,128)(2,1)S(1)}, u32[]{:S(2)}, u32[]{:S(2)}) collective-permute-start(bf16[3,32,1024]{2,1,0:T(8,128)(2,1)S(1)} %pad_maximum_fusion), channel_id=1, source_target_pairs={{0,2},{1,3},{2,0},{3,1},{4,6},{5,7},{6,4},{7,5},{8,10},{9,11},{10,... | collective-permute-start | bytes 589832 | tf_op jit(solution)/shard_map/ppermute | solution.py:119
  14.9 0.0 collective-permute-done
  14.9 4.2 %collective-permute-done.4 = bf16[3,32,1024]{2,1,0:T(8,128)(2,1)S(1)} collective-permute-done((bf16[3,32,1024]{2,1,0:T(8,128)(2,1)S(1)}, bf16[3,32,1024]{2,1,0:T(8,128)(2,1)S(1)}, u32[]{:S(2)}, u32[]{:S(2)}) %collective-permute-start.4) | collective-permute-done | bytes 196640 | tf_op jit(solution)/shard_map/ppermute | solution.py:119
  19.1 0.1 collective-permute-start.5
  19.2 1.9 %collective-permute-done.5.other_ref = bf16[8,32,1024]{2,1,0:T(8,128)(2,1)S(1)} collective-permute-done((bf16[8,32,1024]{2,1,0:T(8,128)(2,1)S(1)}, bf16[8,32,1024]{2,1,0:T(8,128)(2,1)S(1)}, u32[]{:S(2)}, u32[]{:S(2)}) %collective-permute-start.5) | collective-permute-done | bytes 524320 | tf_op jit(solution)/shard_map/ppermute | solution.py:119
  21.1 24.8 %shard_map.28 = f32[1024,16384]{1,0:T(8,128)} custom-call(bf16[8,32,1024]{2,1,0:T(8,128)(2,1)S(1)} %slice_dynamic-update-slice_fusion.mine_ref, bf16[8,32,1024]{2,1,0:T(8,128)(2,1)S(1)} %collective-permute-done.5.other_ref), custom_call_target="tpu_custom_call" | custom-call | flops 1073741824 | bytes 67108864 | tf_op jit(solution)/shard_map/pallas_call | solution.py:96
  (8 shorter events, 0.1 us)
Async XLA Ops:
  1.5 7.4 %collective-permute-start.2 = (bf16[32,1024]{1,0:T(8,128)(2,1)S(1)}, bf16[32,1024]{1,0:T(8,128)(2,1)S(1)}, u32[]{:S(2)}, u32[]{:S(2)}) collective-permute-start(bf16[32,1024]{1,0:T(8,128)(2,1)S(1)} %get-tuple-element.6), channel_id=1, source_target_pairs={{0,8},{1,9},{2,10},{3,11},{4,12},{5,13},{6,14},{7,15},{8,0},{9,1},... | collective-permute-start | bytes 196616 | tf_op jit(solution)/shard_map/ppermute | solution.py:119
  5.7 4.3 %collective-permute-start.1 = (bf16[32,1024]{1,0:T(8,128)(2,1)S(1)}, bf16[32,1024]{1,0:T(8,128)(2,1)S(1)}, u32[]{:S(2)}, u32[]{:S(2)}) collective-permute-start(bf16[32,1024]{1,0:T(8,128)(2,1)S(1)} %get-tuple-element.6), channel_id=1, source_target_pairs={{0,4},{1,5},{2,6},{3,7},{4,0},{5,1},{6,2},{7,3},{8,12},{9,13},{10,... | collective-permute-start | bytes 196616 | tf_op jit(solution)/shard_map/ppermute | solution.py:119
  7.2 6.1 %collective-permute-start.3 = (bf16[32,1024]{1,0:T(8,128)(2,1)S(1)}, bf16[32,1024]{1,0:T(8,128)(2,1)S(1)}, u32[]{:S(2)}, u32[]{:S(2)}) collective-permute-start(bf16[32,1024]{1,0:T(8,128)(2,1)S(1)} %get-tuple-element.6), channel_id=1, source_target_pairs={{0,12},{1,13},{2,14},{3,15},{4,8},{5,9},{6,10},{7,11},{8,4},{9,5},... | collective-permute-start | bytes 196616 | tf_op jit(solution)/shard_map/ppermute | solution.py:119
  7.2 7.6 %collective-permute-start = (bf16[32,1024]{1,0:T(8,128)(2,1)S(1)}, bf16[32,1024]{1,0:T(8,128)(2,1)S(1)}, u32[]{:S(2)}, u32[]{:S(2)}) collective-permute-start(bf16[32,1024]{1,0:T(8,128)(2,1)S(1)} %get-tuple-element.6), channel_id=1, source_target_pairs={{0,2},{1,3},{2,0},{3,1},{4,6},{5,7},{6,4},{7,5},{8,10},{9,11},{10,... | collective-permute-start | bytes 196616 | tf_op jit(solution)/shard_map/ppermute | solution.py:119
  13.3 5.7 %collective-permute-start.4 = (bf16[3,32,1024]{2,1,0:T(8,128)(2,1)S(1)}, bf16[3,32,1024]{2,1,0:T(8,128)(2,1)S(1)}, u32[]{:S(2)}, u32[]{:S(2)}) collective-permute-start(bf16[3,32,1024]{2,1,0:T(8,128)(2,1)S(1)} %pad_maximum_fusion), channel_id=1, source_target_pairs={{0,2},{1,3},{2,0},{3,1},{4,6},{5,7},{6,4},{7,5},{8,10},{9,11},{10,... | collective-permute-start | bytes 589832 | tf_op jit(solution)/shard_map/ppermute | solution.py:119
  19.1 2.0 %collective-permute-start.5 = (bf16[8,32,1024]{2,1,0:T(8,128)(2,1)S(1)}, bf16[8,32,1024]{2,1,0:T(8,128)(2,1)S(1)}, u32[]{:S(2)}, u32[]{:S(2)}) collective-permute-start(bf16[8,32,1024]{2,1,0:T(8,128)(2,1)S(1)} %slice_dynamic-update-slice_fusion.mine_ref), channel_id=1, source_target_pairs={{0,1},{1,0},{2,3},{3,2},{4,5},{5,4},{6,7},{7,6},{8,9},{9,8},{10,11... | collective-permute-start | bytes 1572872 | tf_op jit(solution)/shard_map/ppermute | solution.py:119

commit v2 on v1

--- a/solution.py
+++ b/solution.py
@@ -10,6 +10,7 @@
 LANES = 128
 CHUNK = 512
 BUFFERS = 4
+UNROLL = 8
 
 
 def butterfly(terms):
@@ -35,6 +36,18 @@
     return value & 1
 
 
+def in_turns(steps):
+    unroll = min(UNROLL, steps)
+
+    def run(body):
+        @pl.loop(0, steps // unroll)
+        def _(turn):
+            for i in range(unroll):
+                body(turn * unroll + i)
+
+    return run
+
+
 def hessian_kernel(ranks, mine_ref, other_ref, out_ref, wide, rotated, own_rows, tiles, sems):
     me = lax.axis_index("tensor")
     half, tokens, columns = mine_ref.shape
@@ -46,7 +59,7 @@
     inner = ((1 - 2 * odd_bits(row & col, LANES)).astype(jnp.float32) * (1.0 / LANES)).astype(jnp.bfloat16)
     for offset, ref in ((0, mine_ref), (1, other_ref)):
 
-        @pl.loop(0, half)
+        @in_turns(half)
         def _(k):
             block = ref[k]
             stacked = jnp.concatenate([block[:, j * LANES : (j + 1) * LANES] for j in range(local)], axis=0)
@@ -57,15 +70,16 @@
 
     signs = [(1 - 2 * odd_bits(me & m, ranks)).astype(jnp.float32) for m in range(ranks)]
 
-    @pl.loop(0, local)
-    def _(j):
-        @pl.loop(0, tokens // 16)
-        def _(t):
-            rows = pl.ds(pl.multiple_of(t * 16, 16), 16)
-            terms = butterfly([wide[k, j, rows, :] for k in range(ranks)])
-            for m in range(ranks):
-                at = pl.ds(pl.multiple_of((m * local + j) * LANES, LANES), LANES)
-                rotated[rows, at] = (terms[m] * signs[m]).astype(jnp.bfloat16)
+    pieces = tokens // 16
+
+    @in_turns(local * pieces)
+    def _(piece):
+        j = piece // pieces
+        rows = pl.ds(pl.multiple_of(piece % pieces * 16, 16), 16)
+        terms = butterfly([wide[k, j, rows, :] for k in range(ranks)])
+        for m in range(ranks):
+            at = pl.ds(pl.multiple_of((m * local + j) * LANES, LANES), LANES)
+            rotated[rows, at] = (terms[m] * signs[m]).astype(jnp.bfloat16)
 
     own_rows[...] = rotated[:, pl.ds(pl.multiple_of(me * columns, LANES), columns)].T
 

time: 46.1 us -> 44.1 us (0.957)
  Pallas kernels: 24.8 us -> 22.8 us
    pallas_call x1, Pallas kernels: 24.8 us -> 22.8 us  [hessian_rows(): pl.pallas_call(functools.partial(hessian_kernel, ranks), in_specs=[pl.Blo...]
where the time goes in v2:
time: 44.1 us; the launch traced here: 43.9 us
  Pallas kernels  22.8 us (52%)
  waiting for transfers between devices  10.4 us (24%)
  starting transfers between devices  9.02 us (20%)
  other arithmetic  1.57 us (4%)
    pallas_call x1, Pallas kernels, hessian_rows(): pl.pallas_call(functools.partial(hessian_kernel, ranks), in_specs=[pl.Blo...  22.8 us
    ppermute x6, waiting for transfers between devices, from_partner(): return lax.ppermute(x, 'tensor', [(i, i ^ k) for i in range(ranks)])  10.4 us
    ppermute x6, starting transfers between devices, from_partner(): return lax.ppermute(x, 'tensor', [(i, i ^ k) for i in range(ranks)])  9.02 us
  transfers between devices with their start and end apart: 6, of which 4 were waited for; matrix products, arithmetic and copies ran while one was open for 0% of the time, Pallas kernels for 0%

profile of v2, /device:TPU:0, one launch (start us, length us, event | category | flops | bytes accessed | tf_op | source)
XLA Modules:
  0.0 43.9 jit_solution(8573797302895085664)
XLA Ops:
  0.0 0.7 %convert_element_type.3 = bf16[1024]{0:T(1024)(128)(2,1)S(1)} convert(s32[1024]{0:T(1024)} %param.3) | non-fusion elementwise | flops 1024 | bytes 6144 | tf_op jit(solution)/shard_map/convert_element_type | solution.py:130
  0.7 0.9 %bitcast_dynamic-update-slice_fusion.1 = (bf16[8,32,1024]{2,1,0:T(8,128)(2,1)S(1)}, bf16[32,1024]{1,0:T(8,128)(2,1)S(1)}) fusion(bf16[32,1024]{1,0:T(8,128)(2,1)} %param.2, bf16[1024]{0:T(1024)(128)(2,1)S(1)} %convert_element_type.3), kind=kLoop, calls=%fused_computation.5 | loop fusion | flops 131071 | bytes 198656
  1.5 4.1 %collective-permute-start.2 = (bf16[32,1024]{1,0:T(8,128)(2,1)S(1)}, bf16[32,1024]{1,0:T(8,128)(2,1)S(1)}, u32[]{:S(2)}, u32[]{:S(2)}) collective-permute-start(bf16[32,1024]{1,0:T(8,128)(2,1)S(1)} %get-tuple-element.6), channel_id=1, source_target_pairs={{0,8},{1,9},{2,10},{3,11},{4,12},{5,13},{6,14},{7,15},{8,0},{9,1},... | collective-permute-start | bytes 196616 | tf_op jit(solution)/shard_map/ppermute | solution.py:133
  5.7 1.6 %collective-permute-start.1 = (bf16[32,1024]{1,0:T(8,128)(2,1)S(1)}, bf16[32,1024]{1,0:T(8,128)(2,1)S(1)}, u32[]{:S(2)}, u32[]{:S(2)}) collective-permute-start(bf16[32,1024]{1,0:T(8,128)(2,1)S(1)} %get-tuple-element.6), channel_id=1, source_target_pairs={{0,4},{1,5},{2,6},{3,7},{4,0},{5,1},{6,2},{7,3},{8,12},{9,13},{10,... | collective-permute-start | bytes 196616 | tf_op jit(solution)/shard_map/ppermute | solution.py:133
  7.2 0.0 collective-permute-start.3
  7.2 1.7 %collective-permute-start = (bf16[32,1024]{1,0:T(8,128)(2,1)S(1)}, bf16[32,1024]{1,0:T(8,128)(2,1)S(1)}, u32[]{:S(2)}, u32[]{:S(2)}) collective-permute-start(bf16[32,1024]{1,0:T(8,128)(2,1)S(1)} %get-tuple-element.6), channel_id=1, source_target_pairs={{0,2},{1,3},{2,0},{3,1},{4,6},{5,7},{6,4},{7,5},{8,10},{9,11},{10,... | collective-permute-start | bytes 196616 | tf_op jit(solution)/shard_map/ppermute | solution.py:133
  8.9 0.0 collective-permute-done.2
  8.9 1.0 %collective-permute-done.1 = bf16[32,1024]{1,0:T(8,128)(2,1)S(1)} collective-permute-done((bf16[32,1024]{1,0:T(8,128)(2,1)S(1)}, bf16[32,1024]{1,0:T(8,128)(2,1)S(1)}, u32[]{:S(2)}, u32[]{:S(2)}) %collective-permute-start.1) | collective-permute-done | bytes 65568 | tf_op jit(solution)/shard_map/ppermute | solution.py:133
  9.9 3.4 %collective-permute-done.3 = bf16[32,1024]{1,0:T(8,128)(2,1)S(1)} collective-permute-done((bf16[32,1024]{1,0:T(8,128)(2,1)S(1)}, bf16[32,1024]{1,0:T(8,128)(2,1)S(1)}, u32[]{:S(2)}, u32[]{:S(2)}) %collective-permute-start.3) | collective-permute-done | bytes 65568 | tf_op jit(solution)/shard_map/ppermute | solution.py:133
  13.3 1.6 %collective-permute-start.4 = (bf16[3,32,1024]{2,1,0:T(8,128)(2,1)S(1)}, bf16[3,32,1024]{2,1,0:T(8,128)(2,1)S(1)}, u32[]{:S(2)}, u32[]{:S(2)}) collective-permute-start(bf16[3,32,1024]{2,1,0:T(8,128)(2,1)S(1)} %pad_maximum_fusion), channel_id=1, source_target_pairs={{0,2},{1,3},{2,0},{3,1},{4,6},{5,7},{6,4},{7,5},{8,10},{9,11},{10,... | collective-permute-start | bytes 589832 | tf_op jit(solution)/shard_map/ppermute | solution.py:133
  14.9 0.0 collective-permute-done
  14.9 4.2 %collective-permute-done.4 = bf16[3,32,1024]{2,1,0:T(8,128)(2,1)S(1)} collective-permute-done((bf16[3,32,1024]{2,1,0:T(8,128)(2,1)S(1)}, bf16[3,32,1024]{2,1,0:T(8,128)(2,1)S(1)}, u32[]{:S(2)}, u32[]{:S(2)}) %collective-permute-start.4) | collective-permute-done | bytes 196640 | tf_op jit(solution)/shard_map/ppermute | solution.py:133
  19.1 0.1 collective-permute-start.5
  19.2 1.9 %collective-permute-done.5.other_ref = bf16[8,32,1024]{2,1,0:T(8,128)(2,1)S(1)} collective-permute-done((bf16[8,32,1024]{2,1,0:T(8,128)(2,1)S(1)}, bf16[8,32,1024]{2,1,0:T(8,128)(2,1)S(1)}, u32[]{:S(2)}, u32[]{:S(2)}) %collective-permute-start.5) | collective-permute-done | bytes 524320 | tf_op jit(solution)/shard_map/ppermute | solution.py:133
  21.1 22.8 %shard_map.28 = f32[1024,16384]{1,0:T(8,128)} custom-call(bf16[8,32,1024]{2,1,0:T(8,128)(2,1)S(1)} %slice_dynamic-update-slice_fusion.mine_ref, bf16[8,32,1024]{2,1,0:T(8,128)(2,1)S(1)} %collective-permute-done.5.other_ref), custom_call_target="tpu_custom_call" | custom-call | flops 1073741824 | bytes 67108864 | tf_op jit(solution)/shard_map/pallas_call | solution.py:110
  (8 shorter events, 0.1 us)
Async XLA Ops:
  1.5 7.4 %collective-permute-start.2 = (bf16[32,1024]{1,0:T(8,128)(2,1)S(1)}, bf16[32,1024]{1,0:T(8,128)(2,1)S(1)}, u32[]{:S(2)}, u32[]{:S(2)}) collective-permute-start(bf16[32,1024]{1,0:T(8,128)(2,1)S(1)} %get-tuple-element.6), channel_id=1, source_target_pairs={{0,8},{1,9},{2,10},{3,11},{4,12},{5,13},{6,14},{7,15},{8,0},{9,1},... | collective-permute-start | bytes 196616 | tf_op jit(solution)/shard_map/ppermute | solution.py:133
  5.7 4.3 %collective-permute-start.1 = (bf16[32,1024]{1,0:T(8,128)(2,1)S(1)}, bf16[32,1024]{1,0:T(8,128)(2,1)S(1)}, u32[]{:S(2)}, u32[]{:S(2)}) collective-permute-start(bf16[32,1024]{1,0:T(8,128)(2,1)S(1)} %get-tuple-element.6), channel_id=1, source_target_pairs={{0,4},{1,5},{2,6},{3,7},{4,0},{5,1},{6,2},{7,3},{8,12},{9,13},{10,... | collective-permute-start | bytes 196616 | tf_op jit(solution)/shard_map/ppermute | solution.py:133
  7.2 6.1 %collective-permute-start.3 = (bf16[32,1024]{1,0:T(8,128)(2,1)S(1)}, bf16[32,1024]{1,0:T(8,128)(2,1)S(1)}, u32[]{:S(2)}, u32[]{:S(2)}) collective-permute-start(bf16[32,1024]{1,0:T(8,128)(2,1)S(1)} %get-tuple-element.6), channel_id=1, source_target_pairs={{0,12},{1,13},{2,14},{3,15},{4,8},{5,9},{6,10},{7,11},{8,4},{9,5},... | collective-permute-start | bytes 196616 | tf_op jit(solution)/shard_map/ppermute | solution.py:133
  7.2 7.6 %collective-permute-start = (bf16[32,1024]{1,0:T(8,128)(2,1)S(1)}, bf16[32,1024]{1,0:T(8,128)(2,1)S(1)}, u32[]{:S(2)}, u32[]{:S(2)}) collective-permute-start(bf16[32,1024]{1,0:T(8,128)(2,1)S(1)} %get-tuple-element.6), channel_id=1, source_target_pairs={{0,2},{1,3},{2,0},{3,1},{4,6},{5,7},{6,4},{7,5},{8,10},{9,11},{10,... | collective-permute-start | bytes 196616 | tf_op jit(solution)/shard_map/ppermute | solution.py:133
  13.3 5.7 %collective-permute-start.4 = (bf16[3,32,1024]{2,1,0:T(8,128)(2,1)S(1)}, bf16[3,32,1024]{2,1,0:T(8,128)(2,1)S(1)}, u32[]{:S(2)}, u32[]{:S(2)}) collective-permute-start(bf16[3,32,1024]{2,1,0:T(8,128)(2,1)S(1)} %pad_maximum_fusion), channel_id=1, source_target_pairs={{0,2},{1,3},{2,0},{3,1},{4,6},{5,7},{6,4},{7,5},{8,10},{9,11},{10,... | collective-permute-start | bytes 589832 | tf_op jit(solution)/shard_map/ppermute | solution.py:133
  19.1 2.0 %collective-permute-start.5 = (bf16[8,32,1024]{2,1,0:T(8,128)(2,1)S(1)}, bf16[8,32,1024]{2,1,0:T(8,128)(2,1)S(1)}, u32[]{:S(2)}, u32[]{:S(2)}) collective-permute-start(bf16[8,32,1024]{2,1,0:T(8,128)(2,1)S(1)} %slice_dynamic-update-slice_fusion.mine_ref), channel_id=1, source_target_pairs={{0,1},{1,0},{2,3},{3,2},{4,5},{5,4},{6,7},{7,6},{8,9},{9,8},{10,11... | collective-permute-start | bytes 1572872 | tf_op jit(solution)/shard_map/ppermute | solution.py:133

commit v3 on v2

--- a/solution.py
+++ b/solution.py
@@ -132,14 +132,18 @@
     def from_partner(x, k):
         return lax.ppermute(x, "tensor", [(i, i ^ k) for i in range(ranks)])
 
-    far = range(4, ranks, 4)
+    def cross(ks):
+        crossed = from_partner(jnp.stack([blocks[k] for k in ks]), 2)
+        for i, k in enumerate(ks):
+            blocks[k + 2] = crossed[i]
+
+    first = ranks // 2
+    rest = [k for k in range(ranks - 4, 0, -4) if k != first]
     blocks = {0: flipped}
-    for k in far:
+    for k in [first] + rest:
         blocks[k] = from_partner(flipped, k)
-    blocks[2] = from_partner(flipped, 2)
-    crossed = from_partner(jnp.stack([blocks[k] for k in far]), 2)
-    for i, k in enumerate(far):
-        blocks[k + 2] = crossed[i]
+    cross([0, first])
+    cross(rest)
     mine = jnp.stack([blocks[k] for k in range(0, ranks, 2)])
     return hessian_rows(ranks, mine, from_partner(mine, 1))
 

time: 44.1 us -> 42.3 us (0.959)
  waiting for transfers between devices: 10.4 us -> 7.72 us
  starting transfers between devices: 9.02 us -> 9.84 us
    ppermute x6, waiting for transfers between devices: 10.4 us -> 7.72 us  [from_partner(): return lax.ppermute(x, 'tensor', [(i, i ^ k) for i in range(ranks)])]
    ppermute x6, starting transfers between devices: 9.02 us -> 9.84 us  [from_partner(): return lax.ppermute(x, 'tensor', [(i, i ^ k) for i in range(ranks)])]
where the time goes in v3:
time: 42.3 us; the launch traced here: 42.1 us
  Pallas kernels  22.8 us (54%)
  starting transfers between devices  9.84 us (23%)
  waiting for transfers between devices  7.72 us (18%)
  other arithmetic  1.57 us (4%)
    pallas_call x1, Pallas kernels, hessian_rows(): pl.pallas_call(functools.partial(hessian_kernel, ranks), in_specs=[pl.Blo...  22.8 us
    ppermute x6, starting transfers between devices, from_partner(): return lax.ppermute(x, 'tensor', [(i, i ^ k) for i in range(ranks)])  9.84 us
    ppermute x6, waiting for transfers between devices, from_partner(): return lax.ppermute(x, 'tensor', [(i, i ^ k) for i in range(ranks)])  7.72 us
    unnamed x1, other arithmetic  0.86 us
  transfers between devices with their start and end apart: 6, of which 4 were waited for; matrix products, arithmetic and copies ran while one was open for 0% of the time, Pallas kernels for 0%

profile of v3, /device:TPU:0, one launch (start us, length us, event | category | flops | bytes accessed | tf_op | source)
XLA Modules:
  0.0 42.1 jit_solution(2483905950626240253)
XLA Ops:
  0.0 0.7 %convert_element_type.3 = bf16[1024]{0:T(1024)(128)(2,1)S(1)} convert(s32[1024]{0:T(1024)} %param.3) | non-fusion elementwise | flops 1024 | bytes 6144 | tf_op jit(solution)/shard_map/convert_element_type | solution.py:130
  0.7 0.9 %constant_dynamic-update-slice_fusion.3 = (bf16[8,32,1024]{2,1,0:T(8,128)(2,1)S(1)}, bf16[32,1024]{1,0:T(8,128)(2,1)S(1)}) fusion(bf16[32,1024]{1,0:T(8,128)(2,1)} %param.2, bf16[1024]{0:T(1024)(128)(2,1)S(1)} %convert_element_type.3), kind=kLoop, calls=%fused_computation.10 | loop fusion | flops 131071 | bytes 198656
  1.5 4.1 %collective-permute-start = (bf16[32,1024]{1,0:T(8,128)(2,1)S(1)}, bf16[32,1024]{1,0:T(8,128)(2,1)S(1)}, u32[]{:S(2)}, u32[]{:S(2)}) collective-permute-start(bf16[32,1024]{1,0:T(8,128)(2,1)S(1)} %get-tuple-element.6), channel_id=1, source_target_pairs={{0,8},{1,9},{2,10},{3,11},{4,12},{5,13},{6,14},{7,15},{8,0},{9,1},... | collective-permute-start | bytes 196616 | tf_op jit(solution)/shard_map/ppermute | solution.py:133
  5.7 1.3 %collective-permute-start.3 = (bf16[32,1024]{1,0:T(8,128)(2,1)S(1)}, bf16[32,1024]{1,0:T(8,128)(2,1)S(1)}, u32[]{:S(2)}, u32[]{:S(2)}) collective-permute-start(bf16[32,1024]{1,0:T(8,128)(2,1)S(1)} %get-tuple-element.6), channel_id=1, source_target_pairs={{0,12},{1,13},{2,14},{3,15},{4,8},{5,9},{6,10},{7,11},{8,4},{9,5},... | collective-permute-start | bytes 196616 | tf_op jit(solution)/shard_map/ppermute | solution.py:133
  7.0 0.2 collective-permute-start.2
  7.2 2.2 %collective-permute-done = bf16[32,1024]{1,0:T(8,128)(2,1)S(1)} collective-permute-done((bf16[32,1024]{1,0:T(8,128)(2,1)S(1)}, bf16[32,1024]{1,0:T(8,128)(2,1)S(1)}, u32[]{:S(2)}, u32[]{:S(2)}) %collective-permute-start) | collective-permute-done | bytes 65568 | tf_op jit(solution)/shard_map/ppermute | solution.py:133
  9.4 2.6 %collective-permute-start.1 = (bf16[2,32,1024]{2,1,0:T(8,128)(2,1)S(1)}, bf16[2,32,1024]{2,1,0:T(8,128)(2,1)S(1)}, u32[]{:S(2)}, u32[]{:S(2)}) collective-permute-start(bf16[2,32,1024]{2,1,0:T(8,128)(2,1)S(1)} %pad_maximum_fusion), channel_id=1, source_target_pairs={{0,2},{1,3},{2,0},{3,1},{4,6},{5,7},{6,4},{7,5},{8,10},{9,11},{10,... | collective-permute-start | bytes 393224 | tf_op jit(solution)/shard_map/ppermute | solution.py:133
  12.0 0.0 collective-permute-done.3
  12.0 0.0 collective-permute-done.2
  12.0 1.5 %collective-permute-start.4 = (bf16[2,32,1024]{2,1,0:T(8,128)(2,1)S(1)}, bf16[2,32,1024]{2,1,0:T(8,128)(2,1)S(1)}, u32[]{:S(2)}, u32[]{:S(2)}) collective-permute-start(bf16[2,32,1024]{2,1,0:T(8,128)(2,1)S(1)} %pad_maximum_fusion.1), channel_id=1, source_target_pairs={{0,2},{1,3},{2,0},{3,1},{4,6},{5,7},{6,4},{7,5},{8,10},{9,11},{10,... | collective-permute-start | bytes 393224 | tf_op jit(solution)/shard_map/ppermute | solution.py:133
  13.5 2.2 %collective-permute-done.1 = bf16[2,32,1024]{2,1,0:T(8,128)(2,1)S(1)} collective-permute-done((bf16[2,32,1024]{2,1,0:T(8,128)(2,1)S(1)}, bf16[2,32,1024]{2,1,0:T(8,128)(2,1)S(1)}, u32[]{:S(2)}, u32[]{:S(2)}) %collective-permute-start.1) | collective-permute-done | bytes 131104 | tf_op jit(solution)/shard_map/ppermute | solution.py:133
  15.8 1.4 %collective-permute-done.4 = bf16[2,32,1024]{2,1,0:T(8,128)(2,1)S(1)} collective-permute-done((bf16[2,32,1024]{2,1,0:T(8,128)(2,1)S(1)}, bf16[2,32,1024]{2,1,0:T(8,128)(2,1)S(1)}, u32[]{:S(2)}, u32[]{:S(2)}) %collective-permute-start.4) | collective-permute-done | bytes 131104 | tf_op jit(solution)/shard_map/ppermute | solution.py:133
  17.3 0.1 collective-permute-start.5
  17.3 1.9 %collective-permute-done.5.other_ref = bf16[8,32,1024]{2,1,0:T(8,128)(2,1)S(1)} collective-permute-done((bf16[8,32,1024]{2,1,0:T(8,128)(2,1)S(1)}, bf16[8,32,1024]{2,1,0:T(8,128)(2,1)S(1)}, u32[]{:S(2)}, u32[]{:S(2)}) %collective-permute-start.5) | collective-permute-done | bytes 524320 | tf_op jit(solution)/shard_map/ppermute | solution.py:133
  19.2 22.8 %shard_map.28 = f32[1024,16384]{1,0:T(8,128)} custom-call(bf16[8,32,1024]{2,1,0:T(8,128)(2,1)S(1)} %slice_dynamic-update-slice_fusion.mine_ref, bf16[8,32,1024]{2,1,0:T(8,128)(2,1)S(1)} %collective-permute-done.5.other_ref), custom_call_target="tpu_custom_call" | custom-call | flops 1073741824 | bytes 67108864 | tf_op jit(solution)/shard_map/pallas_call | solution.py:110
  (9 shorter events, 0.1 us)
Async XLA Ops:
  1.5 7.9 %collective-permute-start = (bf16[32,1024]{1,0:T(8,128)(2,1)S(1)}, bf16[32,1024]{1,0:T(8,128)(2,1)S(1)}, u32[]{:S(2)}, u32[]{:S(2)}) collective-permute-start(bf16[32,1024]{1,0:T(8,128)(2,1)S(1)} %get-tuple-element.6), channel_id=1, source_target_pairs={{0,8},{1,9},{2,10},{3,11},{4,12},{5,13},{6,14},{7,15},{8,0},{9,1},... | collective-permute-start | bytes 196616 | tf_op jit(solution)/shard_map/ppermute | solution.py:133
  5.7 6.4 %collective-permute-start.3 = (bf16[32,1024]{1,0:T(8,128)(2,1)S(1)}, bf16[32,1024]{1,0:T(8,128)(2,1)S(1)}, u32[]{:S(2)}, u32[]{:S(2)}) collective-permute-start(bf16[32,1024]{1,0:T(8,128)(2,1)S(1)} %get-tuple-element.6), channel_id=1, source_target_pairs={{0,12},{1,13},{2,14},{3,15},{4,8},{5,9},{6,10},{7,11},{8,4},{9,5},... | collective-permute-start | bytes 196616 | tf_op jit(solution)/shard_map/ppermute | solution.py:133
  7.0 5.0 %collective-permute-start.2 = (bf16[32,1024]{1,0:T(8,128)(2,1)S(1)}, bf16[32,1024]{1,0:T(8,128)(2,1)S(1)}, u32[]{:S(2)}, u32[]{:S(2)}) collective-permute-start(bf16[32,1024]{1,0:T(8,128)(2,1)S(1)} %get-tuple-element.6), channel_id=1, source_target_pairs={{0,4},{1,5},{2,6},{3,7},{4,0},{5,1},{6,2},{7,3},{8,12},{9,13},{10,... | collective-permute-start | bytes 196616 | tf_op jit(solution)/shard_map/ppermute | solution.py:133
  9.4 6.4 %collective-permute-start.1 = (bf16[2,32,1024]{2,1,0:T(8,128)(2,1)S(1)}, bf16[2,32,1024]{2,1,0:T(8,128)(2,1)S(1)}, u32[]{:S(2)}, u32[]{:S(2)}) collective-permute-start(bf16[2,32,1024]{2,1,0:T(8,128)(2,1)S(1)} %pad_maximum_fusion), channel_id=1, source_target_pairs={{0,2},{1,3},{2,0},{3,1},{4,6},{5,7},{6,4},{7,5},{8,10},{9,11},{10,... | collective-permute-start | bytes 393224 | tf_op jit(solution)/shard_map/ppermute | solution.py:133
  12.0 5.2 %collective-permute-start.4 = (bf16[2,32,1024]{2,1,0:T(8,128)(2,1)S(1)}, bf16[2,32,1024]{2,1,0:T(8,128)(2,1)S(1)}, u32[]{:S(2)}, u32[]{:S(2)}) collective-permute-start(bf16[2,32,1024]{2,1,0:T(8,128)(2,1)S(1)} %pad_maximum_fusion.1), channel_id=1, source_target_pairs={{0,2},{1,3},{2,0},{3,1},{4,6},{5,7},{6,4},{7,5},{8,10},{9,11},{10,... | collective-permute-start | bytes 393224 | tf_op jit(solution)/shard_map/ppermute | solution.py:133
  17.3 2.0 %collective-permute-start.5 = (bf16[8,32,1024]{2,1,0:T(8,128)(2,1)S(1)}, bf16[8,32,1024]{2,1,0:T(8,128)(2,1)S(1)}, u32[]{:S(2)}, u32[]{:S(2)}) collective-permute-start(bf16[8,32,1024]{2,1,0:T(8,128)(2,1)S(1)} %slice_dynamic-update-slice_fusion.mine_ref), channel_id=1, source_target_pairs={{0,1},{1,0},{2,3},{3,2},{4,5},{5,4},{6,7},{7,6},{8,9},{9,8},{10,11... | collective-permute-start | bytes 1572872 | tf_op jit(solution)/shard_map/ppermute | solution.py:133

commit v4 on v3

v4 whole, which is shorter than its diff:
```python
import functools

import jax
import jax.numpy as jnp
from jax import lax
from jax.experimental import pallas as pl
from jax.experimental.pallas import tpu as pltpu
from jax.sharding import PartitionSpec as P

LANES = 128
CHUNK = 512
BUFFERS = 4
UNROLL = 8


def butterfly(terms):
    step = 1
    while step < len(terms):
        out = list(terms)
        for low in range(len(terms)):
            if not low & step:
                out[low] = terms[low] + terms[low | step]
                out[low | step] = terms[low] - terms[low | step]
        terms = out
        step *= 2
    return terms


def odd_bits(value, order):
    shift = 1
    while shift < order.bit_length():
        shift *= 2
    while shift:
        value = value ^ (value >> shift)
        shift //= 2
    return value & 1


def in_turns(steps):
    def run(body):
        if steps <= UNROLL:
            for i in range(steps):
                body(i)
            return

        @pl.loop(0, steps // UNROLL)
        def _(turn):
            for i in range(UNROLL):
                body(turn * UNROLL + i)

    return run


def rotate_half(blocks_ref, store):
    half, tokens, columns = blocks_ref.shape
    row = lax.broadcasted_iota(jnp.int32, (LANES, LANES), 0)
    col = lax.broadcasted_iota(jnp.int32, (LANES, LANES), 1)
    inner = ((1 - 2 * odd_bits(row & col, LANES)).astype(jnp.float32) * (1.0 / LANES)).astype(jnp.bfloat16)
    size = min(tokens, max(16, 256 // half))
    pieces = tokens // size

    @in_turns(columns // LANES * pieces)
    def _(piece):
        j = piece // pieces
        rows = pl.ds(piece % pieces * size, size)
        lanes = pl.ds(j * LANES, LANES)
        if not isinstance(piece, int):
            rows = pl.ds(pl.multiple_of(piece % pieces * size, 16), size)
            lanes = pl.ds(pl.multiple_of(j * LANES, LANES), LANES)
        stacked = jnp.concatenate([blocks_ref[k, rows, lanes] for k in range(half)], axis=0)
        spread = jnp.dot(stacked, inner, preferred_element_type=jnp.float32)
        store(j, rows, butterfly([spread[k * size : (k + 1) * size] for k in range(half)]))


def half_kernel(mine_ref, out_ref):
    def store(j, rows, terms):
        for m, term in enumerate(terms):
            out_ref[m, j, rows, :] = term

    rotate_half(mine_ref, store)


def hessian_kernel(ranks, half_ref, other_ref, out_ref, wide, rotated, own_rows, tiles, sems):
    me = lax.axis_index("tensor")
    half, tokens, columns = other_ref.shape
    local = columns // LANES
    width = ranks * columns
    turn_width = BUFFERS * CHUNK

    def store(j, rows, terms):
        for m, term in enumerate(terms):
            mine = half_ref[m, j, rows, :]
            wide[2 * m, j, rows, :] = mine + term
            wide[2 * m + 1, j, rows, :] = mine - term

    rotate_half(other_ref, store)

    def finish(m, start):
        sign = (1 - 2 * odd_bits(me & m, ranks)).astype(jnp.float32)
        for e, term in enumerate(butterfly([wide[m, j] for j in range(local)])):
            rotated[:, start + e * LANES : start + (e + 1) * LANES] = (term * sign).astype(jnp.bfloat16)

    finish(me, 0)
    own_rows[...] = rotated[:, :columns].T

    def copy(step, slot):
        at = pl.ds(pl.multiple_of(step * CHUNK, CHUNK), CHUNK)
        return pltpu.make_async_copy(tiles.at[slot], out_ref.at[:, at], sems.at[slot])

    @pl.loop(0, width // turn_width)
    def _(turn):
        for i in range(turn_width // columns):
            finish(turn * (turn_width // columns) + i, i * columns)
        for slot in range(BUFFERS):
            step = turn * BUFFERS + slot

            @pl.when(turn > 0)
            def _():
                copy(step - BUFFERS, slot).wait()

            rows = rotated[:, slot * CHUNK : (slot + 1) * CHUNK]
            tiles[slot] = jnp.dot(own_rows[...], rows, preferred_element_type=jnp.float32) * (1.0 / tokens)
            copy(step, slot).start()

    for slot in range(BUFFERS):
        copy(width // CHUNK - BUFFERS + slot, slot).wait()


def rotate_mine(mine):
    half, tokens, columns = mine.shape
    return pl.pallas_call(
        half_kernel,
        in_specs=[pl.BlockSpec(memory_space=pltpu.VMEM)],
        out_specs=pl.BlockSpec(memory_space=pltpu.VMEM),
        out_shape=jax.ShapeDtypeStruct((half, columns // LANES, tokens, LANES), jnp.float32),
        compiler_params=pltpu.CompilerParams(vmem_limit_bytes=16 * 2**20),
        cost_estimate=pl.CostEstimate(
            flops=2 * half * tokens * columns * LANES, bytes_accessed=6 * half * tokens * columns, transcendentals=0
        ),
    )(mine)


def hessian_rows(ranks, mine, other):
    half, tokens, columns = other.shape
    width = ranks * columns
    return pl.pallas_call(
        functools.partial(hessian_kernel, ranks),
        in_specs=[pl.BlockSpec(memory_space=pltpu.VMEM)] * 2,
        out_specs=pl.BlockSpec(memory_space=pl.ANY),
        out_shape=jax.ShapeDtypeStruct((columns, width), jnp.float32),
        scratch_shapes=[
            pltpu.VMEM((ranks, columns // LANES, tokens, LANES), jnp.float32),
            pltpu.VMEM((tokens, BUFFERS * CHUNK), jnp.bfloat16),
            pltpu.VMEM((columns, tokens), jnp.bfloat16),
            pltpu.VMEM((BUFFERS, columns, CHUNK), jnp.float32),
            pltpu.SemaphoreType.DMA((BUFFERS,)),
        ],
        compiler_params=pltpu.CompilerParams(vmem_limit_bytes=40 * 2**20),
        cost_estimate=pl.CostEstimate(
            flops=2 * tokens * columns * width, bytes_accessed=4 * columns * width, transcendentals=0
        ),
    )(mine, other)


def per_device(ranks, activations, signs):
    sign = jnp.where(activations == 0, 1, lax.broadcast_in_dim(signs, activations.shape, (1,)))
    flipped = activations * sign.astype(jnp.bfloat16)

    def from_partner(x, k):
        return lax.ppermute(x, "tensor", [(i, i ^ k) for i in range(ranks)])

    def cross(ks):
        crossed = from_partner(jnp.stack([blocks[k] for k in ks]), 2)
        for i, k in enumerate(ks):
            blocks[k + 2] = crossed[i]

    first = ranks // 2
    rest = [k for k in range(ranks - 4, 0, -4) if k != first]
    blocks = {0: flipped}
    for k in [first] + rest:
        blocks[k] = from_partner(flipped, k)
    cross([0, first])
    cross(rest)
    mine = jnp.stack([blocks[k] for k in range(0, ranks, 2)])
    return hessian_rows(ranks, rotate_mine(mine), from_partner(mine, 1))


def solution(mesh):
    return jax.shard_map(
        functools.partial(per_device, mesh.shape["tensor"]),
        mesh=mesh,
        in_specs=(P("groups", "tensor"), P("tensor")),
        out_specs=P(("groups", "tensor"), None),
        check_vma=False,
    )
```

time: 42.3 us -> 41 us (0.969)
  other arithmetic: 1.57 us -> 0.9 us
    convert_element_type x1 -> x0, other arithmetic: 0.69 us -> none  [per_device(): flipped = activations * signs.astype(jnp.bfloat16)[None, :]]
    pallas_call x1, Pallas kernels: 22.8 us -> 22.1 us  [hessian_rows(): pl.pallas_call(functools.partial(hessian_kernel, ranks), in_specs=[pl.Blo...]
  transfers between devices with their start and end apart: 6 -> 6, of which waited for: 4 -> 4; matrix products, arithmetic and copies ran while one was open for 0% -> 0% of each run, Pallas kernels for 0% -> 1%
where the time goes in v4:
time: 41 us; the launch traced here: 40.7 us
  Pallas kernels  22.5 us (55%)
  starting transfers between devices  9.84 us (24%)
  waiting for transfers between devices  7.36 us (18%)
  other arithmetic  0.9 us (2%)
    pallas_call x1, Pallas kernels, hessian_rows(): pl.pallas_call(functools.partial(hessian_kernel, ranks), in_specs=[pl.Blo...  22.1 us
    ppermute x6, starting transfers between devices, from_partner(): return lax.ppermute(x, 'tensor', [(i, i ^ k) for i in range(ranks)])  9.84 us
    ppermute x6, waiting for transfers between devices, from_partner(): return lax.ppermute(x, 'tensor', [(i, i ^ k) for i in range(ranks)])  7.36 us
    unnamed x1, other arithmetic  0.87 us
  transfers between devices with their start and end apart: 6, of which 4 were waited for; matrix products, arithmetic and copies ran while one was open for 0% of the time, Pallas kernels for 1%

profile of v4, /device:TPU:0, one launch (start us, length us, event | category | flops | bytes accessed | tf_op | source)
XLA Modules:
  0.0 40.7 jit_solution(8143371482661776708)
XLA Ops:
  0.0 0.9 %constant_dynamic-update-slice_fusion.3 = (bf16[8,32,1024]{2,1,0:T(8,128)(2,1)S(1)}, bf16[32,1024]{1,0:T(8,128)(2,1)S(1)}) fusion(bf16[32,1024]{1,0:T(8,128)(2,1)} %param.2, s32[1024]{0:T(1024)} %param.3), kind=kLoop, calls=%fused_computation.11 | loop fusion | flops 262143 | bytes 200704
  0.9 4.1 %collective-permute-start = (bf16[32,1024]{1,0:T(8,128)(2,1)S(1)}, bf16[32,1024]{1,0:T(8,128)(2,1)S(1)}, u32[]{:S(2)}, u32[]{:S(2)}) collective-permute-start(bf16[32,1024]{1,0:T(8,128)(2,1)S(1)} %get-tuple-element.6), channel_id=1, source_target_pairs={{0,8},{1,9},{2,10},{3,11},{4,12},{5,13},{6,14},{7,15},{8,0},{9,1},... | collective-permute-start | bytes 196616 | tf_op jit(solution)/shard_map/ppermute | solution.py:170
  5.0 1.3 %collective-permute-start.3 = (bf16[32,1024]{1,0:T(8,128)(2,1)S(1)}, bf16[32,1024]{1,0:T(8,128)(2,1)S(1)}, u32[]{:S(2)}, u32[]{:S(2)}) collective-permute-start(bf16[32,1024]{1,0:T(8,128)(2,1)S(1)} %get-tuple-element.6), channel_id=1, source_target_pairs={{0,12},{1,13},{2,14},{3,15},{4,8},{5,9},{6,10},{7,11},{8,4},{9,5},... | collective-permute-start | bytes 196616 | tf_op jit(solution)/shard_map/ppermute | solution.py:170
  6.3 0.2 collective-permute-start.2
  6.6 2.2 %collective-permute-done = bf16[32,1024]{1,0:T(8,128)(2,1)S(1)} collective-permute-done((bf16[32,1024]{1,0:T(8,128)(2,1)S(1)}, bf16[32,1024]{1,0:T(8,128)(2,1)S(1)}, u32[]{:S(2)}, u32[]{:S(2)}) %collective-permute-start) | collective-permute-done | bytes 65568 | tf_op jit(solution)/shard_map/ppermute | solution.py:170
  8.7 2.6 %collective-permute-start.1 = (bf16[2,32,1024]{2,1,0:T(8,128)(2,1)S(1)}, bf16[2,32,1024]{2,1,0:T(8,128)(2,1)S(1)}, u32[]{:S(2)}, u32[]{:S(2)}) collective-permute-start(bf16[2,32,1024]{2,1,0:T(8,128)(2,1)S(1)} %pad_maximum_fusion), channel_id=1, source_target_pairs={{0,2},{1,3},{2,0},{3,1},{4,6},{5,7},{6,4},{7,5},{8,10},{9,11},{10,... | collective-permute-start | bytes 393224 | tf_op jit(solution)/shard_map/ppermute | solution.py:170
  11.3 0.0 collective-permute-done.3
  11.3 0.0 collective-permute-done.2
  11.4 1.5 %collective-permute-start.4 = (bf16[2,32,1024]{2,1,0:T(8,128)(2,1)S(1)}, bf16[2,32,1024]{2,1,0:T(8,128)(2,1)S(1)}, u32[]{:S(2)}, u32[]{:S(2)}) collective-permute-start(bf16[2,32,1024]{2,1,0:T(8,128)(2,1)S(1)} %pad_maximum_fusion.1), channel_id=1, source_target_pairs={{0,2},{1,3},{2,0},{3,1},{4,6},{5,7},{6,4},{7,5},{8,10},{9,11},{10,... | collective-permute-start | bytes 393224 | tf_op jit(solution)/shard_map/ppermute | solution.py:170
  12.9 2.2 %collective-permute-done.1 = bf16[2,32,1024]{2,1,0:T(8,128)(2,1)S(1)} collective-permute-done((bf16[2,32,1024]{2,1,0:T(8,128)(2,1)S(1)}, bf16[2,32,1024]{2,1,0:T(8,128)(2,1)S(1)}, u32[]{:S(2)}, u32[]{:S(2)}) %collective-permute-start.1) | collective-permute-done | bytes 131104 | tf_op jit(solution)/shard_map/ppermute | solution.py:170
  15.1 1.4 %collective-permute-done.4 = bf16[2,32,1024]{2,1,0:T(8,128)(2,1)S(1)} collective-permute-done((bf16[2,32,1024]{2,1,0:T(8,128)(2,1)S(1)}, bf16[2,32,1024]{2,1,0:T(8,128)(2,1)S(1)}, u32[]{:S(2)}, u32[]{:S(2)}) %collective-permute-start.4) | collective-permute-done | bytes 131104 | tf_op jit(solution)/shard_map/ppermute | solution.py:170
  16.6 0.1 collective-permute-start.5
  16.7 0.3 shard_map.28.half_ref
  17.0 1.5 %collective-permute-done.5.other_ref = bf16[8,32,1024]{2,1,0:T(8,128)(2,1)S(1)} collective-permute-done((bf16[8,32,1024]{2,1,0:T(8,128)(2,1)S(1)}, bf16[8,32,1024]{2,1,0:T(8,128)(2,1)S(1)}, u32[]{:S(2)}, u32[]{:S(2)}) %collective-permute-start.5) | collective-permute-done | bytes 524320 | tf_op jit(solution)/shard_map/ppermute | solution.py:170
  18.6 22.1 %shard_map.29 = f32[1024,16384]{1,0:T(8,128)} custom-call(f32[8,8,32,128]{3,2,1,0:T(8,128)S(1)} %shard_map.28.half_ref, bf16[8,32,1024]{2,1,0:T(8,128)(2,1)S(1)} %collective-permute-done.5.other_ref), custom_call_target="tpu_custom_call" | custom-call | flops 1073741824 | bytes 67108864 | tf_op jit(solution)/shard_map/pallas_call | solution.py:146
  (9 shorter events, 0.1 us)
Async XLA Ops:
  0.9 7.9 %collective-permute-start = (bf16[32,1024]{1,0:T(8,128)(2,1)S(1)}, bf16[32,1024]{1,0:T(8,128)(2,1)S(1)}, u32[]{:S(2)}, u32[]{:S(2)}) collective-permute-start(bf16[32,1024]{1,0:T(8,128)(2,1)S(1)} %get-tuple-element.6), channel_id=1, source_target_pairs={{0,8},{1,9},{2,10},{3,11},{4,12},{5,13},{6,14},{7,15},{8,0},{9,1},... | collective-permute-start | bytes 196616 | tf_op jit(solution)/shard_map/ppermute | solution.py:170
  5.0 6.4 %collective-permute-start.3 = (bf16[32,1024]{1,0:T(8,128)(2,1)S(1)}, bf16[32,1024]{1,0:T(8,128)(2,1)S(1)}, u32[]{:S(2)}, u32[]{:S(2)}) collective-permute-start(bf16[32,1024]{1,0:T(8,128)(2,1)S(1)} %get-tuple-element.6), channel_id=1, source_target_pairs={{0,12},{1,13},{2,14},{3,15},{4,8},{5,9},{6,10},{7,11},{8,4},{9,5},... | collective-permute-start | bytes 196616 | tf_op jit(solution)/shard_map/ppermute | solution.py:170
  6.3 5.0 %collective-permute-start.2 = (bf16[32,1024]{1,0:T(8,128)(2,1)S(1)}, bf16[32,1024]{1,0:T(8,128)(2,1)S(1)}, u32[]{:S(2)}, u32[]{:S(2)}) collective-permute-start(bf16[32,1024]{1,0:T(8,128)(2,1)S(1)} %get-tuple-element.6), channel_id=1, source_target_pairs={{0,4},{1,5},{2,6},{3,7},{4,0},{5,1},{6,2},{7,3},{8,12},{9,13},{10,... | collective-permute-start | bytes 196616 | tf_op jit(solution)/shard_map/ppermute | solution.py:170
  8.7 6.4 %collective-permute-start.1 = (bf16[2,32,1024]{2,1,0:T(8,128)(2,1)S(1)}, bf16[2,32,1024]{2,1,0:T(8,128)(2,1)S(1)}, u32[]{:S(2)}, u32[]{:S(2)}) collective-permute-start(bf16[2,32,1024]{2,1,0:T(8,128)(2,1)S(1)} %pad_maximum_fusion), channel_id=1, source_target_pairs={{0,2},{1,3},{2,0},{3,1},{4,6},{5,7},{6,4},{7,5},{8,10},{9,11},{10,... | collective-permute-start | bytes 393224 | tf_op jit(solution)/shard_map/ppermute | solution.py:170
  11.4 5.2 %collective-permute-start.4 = (bf16[2,32,1024]{2,1,0:T(8,128)(2,1)S(1)}, bf16[2,32,1024]{2,1,0:T(8,128)(2,1)S(1)}, u32[]{:S(2)}, u32[]{:S(2)}) collective-permute-start(bf16[2,32,1024]{2,1,0:T(8,128)(2,1)S(1)} %pad_maximum_fusion.1), channel_id=1, source_target_pairs={{0,2},{1,3},{2,0},{3,1},{4,6},{5,7},{6,4},{7,5},{8,10},{9,11},{10,... | collective-permute-start | bytes 393224 | tf_op jit(solution)/shard_map/ppermute | solution.py:170
  16.6 2.0 %collective-permute-start.5 = (bf16[8,32,1024]{2,1,0:T(8,128)(2,1)S(1)}, bf16[8,32,1024]{2,1,0:T(8,128)(2,1)S(1)}, u32[]{:S(2)}, u32[]{:S(2)}) collective-permute-start(bf16[8,32,1024]{2,1,0:T(8,128)(2,1)S(1)} %slice_dynamic-update-slice_fusion.mine_ref), channel_id=1, source_target_pairs={{0,1},{1,0},{2,3},{3,2},{4,5},{5,4},{6,7},{7,6},{8,9},{9,8},{10,11... | collective-permute-start | bytes 1572872 | tf_op jit(solution)/shard_map/ppermute | solution.py:170

commit v5 on v4

--- a/solution.py
+++ b/solution.py
@@ -19,8 +19,13 @@
         out = list(terms)
         for low in range(len(terms)):
             if not low & step:
-                out[low] = terms[low] + terms[low | step]
-                out[low | step] = terms[low] - terms[low | step]
+                first, second = terms[low], terms[low | step]
+                if first is None and second is not None:
+                    out[low], out[low | step] = second, -second
+                elif second is None:
+                    out[low], out[low | step] = first, first
+                else:
+                    out[low], out[low | step] = first + second, first - second
         terms = out
         step *= 2
     return terms
@@ -51,8 +56,8 @@
     return run
 
 
-def rotate_half(blocks_ref, store):
-    half, tokens, columns = blocks_ref.shape
+def rotate_half(half, sources, store):
+    _, tokens, columns = sources[0][0].shape
     row = lax.broadcasted_iota(jnp.int32, (LANES, LANES), 0)
     col = lax.broadcasted_iota(jnp.int32, (LANES, LANES), 1)
     inner = ((1 - 2 * odd_bits(row & col, LANES)).astype(jnp.float32) * (1.0 / LANES)).astype(jnp.bfloat16)
@@ -67,37 +72,50 @@
         if not isinstance(piece, int):
             rows = pl.ds(pl.multiple_of(piece % pieces * size, 16), size)
             lanes = pl.ds(pl.multiple_of(j * LANES, LANES), LANES)
-        stacked = jnp.concatenate([blocks_ref[k, rows, lanes] for k in range(half)], axis=0)
+        stacked = jnp.concatenate([ref[i, rows, lanes] for ref, at in sources for i in range(len(at))], axis=0)
         spread = jnp.dot(stacked, inner, preferred_element_type=jnp.float32)
-        store(j, rows, butterfly([spread[k * size : (k + 1) * size] for k in range(half)]))
-
-
-def half_kernel(mine_ref, out_ref):
+        terms = [None] * half
+        for i, k in enumerate(k for _, at in sources for k in at):
+            terms[k] = spread[i * size : (i + 1) * size]
+        store(j, rows, butterfly(terms))
+
+
+def mine_kernel(early_at, late_at, early_ref, late_ref, out_ref):
     def store(j, rows, terms):
         for m, term in enumerate(terms):
             out_ref[m, j, rows, :] = term
 
-    rotate_half(mine_ref, store)
-
-
-def hessian_kernel(ranks, half_ref, other_ref, out_ref, wide, rotated, own_rows, tiles, sems):
+    rotate_half(len(early_at) + len(late_at), [(early_ref, early_at), (late_ref, late_at)], store)
+
+
+def early_kernel(early_at, half_ref, other_ref, out_ref):
+    def store(j, rows, terms):
+        for m, term in enumerate(terms):
+            mine = half_ref[m, j, rows, :]
+            out_ref[2 * m, j, rows, :] = mine + term
+            out_ref[2 * m + 1, j, rows, :] = mine - term
+
+    rotate_half(half_ref.shape[0], [(other_ref, early_at)], store)
+
+
+def hessian_kernel(ranks, late_at, wide_ref, late_ref, out_ref, late, rotated, own_rows, tiles, sems):
     me = lax.axis_index("tensor")
-    half, tokens, columns = other_ref.shape
+    _, tokens, columns = late_ref.shape
     local = columns // LANES
     width = ranks * columns
     turn_width = BUFFERS * CHUNK
 
     def store(j, rows, terms):
         for m, term in enumerate(terms):
-            mine = half_ref[m, j, rows, :]
-            wide[2 * m, j, rows, :] = mine + term
-            wide[2 * m + 1, j, rows, :] = mine - term
-
-    rotate_half(other_ref, store)
+            late[m, j, rows, :] = term
+
+    rotate_half(ranks // 2, [(late_ref, late_at)], store)
 
     def finish(m, start):
         sign = (1 - 2 * odd_bits(me & m, ranks)).astype(jnp.float32)
-        for e, term in enumerate(butterfly([wide[m, j] for j in range(local)])):
+        side = (1 - 2 * (m & 1)).astype(jnp.float32)
+        terms = [wide_ref[m, j] + side * late[m // 2, j] for j in range(local)]
+        for e, term in enumerate(butterfly(terms)):
             rotated[:, start + e * LANES : start + (e + 1) * LANES] = (term * sign).astype(jnp.bfloat16)
 
     finish(me, 0)
@@ -126,30 +144,44 @@
         copy(width // CHUNK - BUFFERS + slot, slot).wait()
 
 
-def rotate_mine(mine):
-    half, tokens, columns = mine.shape
+def stack_kernel(*refs):
+    for i, ref in enumerate(refs[:-1]):
+        refs[-1][i] = ref[...]
+
+
+def stack(blocks, flops):
+    shape = (len(blocks),) + blocks[0].shape
     return pl.pallas_call(
-        half_kernel,
-        in_specs=[pl.BlockSpec(memory_space=pltpu.VMEM)],
+        stack_kernel,
+        in_specs=[pl.BlockSpec(memory_space=pltpu.VMEM)] * len(blocks),
         out_specs=pl.BlockSpec(memory_space=pltpu.VMEM),
-        out_shape=jax.ShapeDtypeStruct((half, columns // LANES, tokens, LANES), jnp.float32),
+        out_shape=jax.ShapeDtypeStruct(shape, blocks[0].dtype),
         compiler_params=pltpu.CompilerParams(vmem_limit_bytes=16 * 2**20),
-        cost_estimate=pl.CostEstimate(
-            flops=2 * half * tokens * columns * LANES, bytes_accessed=6 * half * tokens * columns, transcendentals=0
-        ),
-    )(mine)
-
-
-def hessian_rows(ranks, mine, other):
-    half, tokens, columns = other.shape
+        cost_estimate=pl.CostEstimate(flops=flops, bytes_accessed=flops // 300, transcendentals=0),
+    )(*blocks)
+
+
+def in_vmem(kernel, shape, *operands):
+    return pl.pallas_call(
+        kernel,
+        in_specs=[pl.BlockSpec(memory_space=pltpu.VMEM)] * len(operands),
+        out_specs=pl.BlockSpec(memory_space=pltpu.VMEM),
+        out_shape=jax.ShapeDtypeStruct(shape, jnp.float32),
+        compiler_params=pltpu.CompilerParams(vmem_limit_bytes=40 * 2**20),
+        cost_estimate=pl.CostEstimate(flops=10**6, bytes_accessed=10**4, transcendentals=0),
+    )(*operands)
+
+
+def hessian_rows(ranks, late_at, wide, late):
+    _, tokens, columns = late.shape
     width = ranks * columns
     return pl.pallas_call(
-        functools.partial(hessian_kernel, ranks),
+        functools.partial(hessian_kernel, ranks, late_at),
         in_specs=[pl.BlockSpec(memory_space=pltpu.VMEM)] * 2,
         out_specs=pl.BlockSpec(memory_space=pl.ANY),
         out_shape=jax.ShapeDtypeStruct((columns, width), jnp.float32),
         scratch_shapes=[
-            pltpu.VMEM((ranks, columns // LANES, tokens, LANES), jnp.float32),
+            pltpu.VMEM((ranks // 2, columns // LANES, tokens, LANES), jnp.float32),
             pltpu.VMEM((tokens, BUFFERS * CHUNK), jnp.bfloat16),
             pltpu.VMEM((columns, tokens), jnp.bfloat16),
             pltpu.VMEM((BUFFERS, columns, CHUNK), jnp.float32),
@@ -159,7 +191,7 @@
         cost_estimate=pl.CostEstimate(
             flops=2 * tokens * columns * width, bytes_accessed=4 * columns * width, transcendentals=0
         ),
-    )(mine, other)
+    )(wide, late)
 
 
 def per_device(ranks, activations, signs):
@@ -169,20 +201,29 @@
     def from_partner(x, k):
         return lax.ppermute(x, "tensor", [(i, i ^ k) for i in range(ranks)])
 
-    def cross(ks):
-        crossed = from_partner(jnp.stack([blocks[k] for k in ks]), 2)
+    def cross(ks, flops):
+        crossed = from_partner(stack([blocks[k] for k in ks], flops), 2)
         for i, k in enumerate(ks):
             blocks[k + 2] = crossed[i]
 
     first = ranks // 2
-    rest = [k for k in range(ranks - 4, 0, -4) if k != first]
+    rest = [k for k in range(4, ranks, 4) if k != first]
     blocks = {0: flipped}
-    for k in [first] + rest:
+    for k in [first] + rest + [2]:
         blocks[k] = from_partner(flipped, k)
-    cross([0, first])
-    cross(rest)
-    mine = jnp.stack([blocks[k] for k in range(0, ranks, 2)])
-    return hessian_rows(ranks, rotate_mine(mine), from_partner(mine, 1))
+    blocks[rest[-1]] = stack([blocks[rest[-1]]], 3 * 10**9)[0]
+    cross([first], 0)
+    cross(rest, 3 * 10**10)
+    late_ks = [k + 2 for k in rest]
+    early_ks = [k for k in range(0, ranks, 2) if k not in late_ks]
+    early_at = [k // 2 for k in early_ks]
+    late_at = [k // 2 for k in late_ks]
+    early = jnp.stack([blocks[k] for k in early_ks])
+    late = stack([blocks[k] for k in late_ks], 3 * 10**10)
+    shape = (activations.shape[1] // LANES, activations.shape[0], LANES)
+    half = in_vmem(functools.partial(mine_kernel, early_at, late_at), (ranks // 2,) + shape, early, late)
+    wide = in_vmem(functools.partial(early_kernel, early_at), (ranks,) + shape, half, from_partner(early, 1))
+    return hessian_rows(ranks, late_at, wide, from_partner(late, 1))
 
 
 def solution(mesh):

time: 41 us -> 39.8 us (0.971)
  waiting for transfers between devices: 7.36 us -> 4.53 us
  starting transfers between devices: 9.84 us -> 11.4 us
    ppermute x6 -> x8, waiting for transfers between devices: 7.36 us -> 4.53 us  [from_partner(): return lax.ppermute(x, 'tensor', [(i, i ^ k) for i in range(ranks)])]
    ppermute x6 -> x8, starting transfers between devices: 9.84 us -> 11.4 us  [from_partner(): return lax.ppermute(x, 'tensor', [(i, i ^ k) for i in range(ranks)])]
    pallas_call x2 -> x7, Pallas kernels: 22.5 us -> 22.8 us  [the longest x1 21.9 us: hessian_rows(): pl.pallas_call(functools.partial(hessian_kernel, ranks, late_at), in_spec...]
  transfers between devices with their start and end apart: 6 -> 8, of which waited for: 4 -> 4; matrix products, arithmetic and copies ran while one was open for 0% -> 0% of each run, Pallas kernels for 1% -> 2%
where the time goes in v5:
time: 39.8 us; the launch traced here: 39.7 us
  Pallas kernels  22.8 us (57%)
  starting transfers between devices  11.4 us (29%)
  waiting for transfers between devices  4.53 us (11%)
  other arithmetic  0.87 us (2%)
    pallas_call x1, Pallas kernels, hessian_rows(): pl.pallas_call(functools.partial(hessian_kernel, ranks, late_at), in_spec...  21.9 us
    ppermute x8, starting transfers between devices, from_partner(): return lax.ppermute(x, 'tensor', [(i, i ^ k) for i in range(ranks)])  11.4 us
    ppermute x8, waiting for transfers between devices, from_partner(): return lax.ppermute(x, 'tensor', [(i, i ^ k) for i in range(ranks)])  4.53 us
    unnamed x1, other arithmetic  0.87 us
    pallas_call x2, Pallas kernels, in_vmem(): pl.pallas_call(kernel, in_specs=[pl.BlockSpec(memory_space=pltpu.VMEM)] *...  0.83 us
  transfers between devices with their start and end apart: 8, of which 4 were waited for; matrix products, arithmetic and copies ran while one was open for 0% of the time, Pallas kernels for 2%

profile of v5, /device:TPU:0, one launch (start us, length us, event | category | flops | bytes accessed | tf_op | source)
XLA Modules:
  0.0 39.7 jit_solution(12056992224388512216)
XLA Ops:
  0.0 0.9 %bitcast_dynamic-update-slice_fusion.3 = (bf16[6,32,1024]{2,1,0:T(8,128)(2,1)S(1)}, bf16[32,1024]{1,0:T(8,128)(2,1)S(1)}) fusion(bf16[32,1024]{1,0:T(8,128)(2,1)} %param.2, s32[1024]{0:T(1024)} %param.3), kind=kLoop, calls=%fused_computation.7 | loop fusion | flops 262143 | bytes 200704
  0.9 4.1 %collective-permute-start.2 = (bf16[32,1024]{1,0:T(8,128)(2,1)S(1)}, bf16[32,1024]{1,0:T(8,128)(2,1)S(1)}, u32[]{:S(2)}, u32[]{:S(2)}) collective-permute-start(bf16[32,1024]{1,0:T(8,128)(2,1)S(1)} %get-tuple-element.6), channel_id=1, source_target_pairs={{0,8},{1,9},{2,10},{3,11},{4,12},{5,13},{6,14},{7,15},{8,0},{9,1},... | collective-permute-start | bytes 196616 | tf_op jit(solution)/shard_map/ppermute | solution.py:202
  5.0 1.3 %collective-permute-start.4 = (bf16[32,1024]{1,0:T(8,128)(2,1)S(1)}, bf16[32,1024]{1,0:T(8,128)(2,1)S(1)}, u32[]{:S(2)}, u32[]{:S(2)}) collective-permute-start(bf16[32,1024]{1,0:T(8,128)(2,1)S(1)} %get-tuple-element.6), channel_id=1, source_target_pairs={{0,12},{1,13},{2,14},{3,15},{4,8},{5,9},{6,10},{7,11},{8,4},{9,5},... | collective-permute-start | bytes 196616 | tf_op jit(solution)/shard_map/ppermute | solution.py:202
  6.3 0.2 collective-permute-start.1
  6.6 1.5 %collective-permute-start = (bf16[32,1024]{1,0:T(8,128)(2,1)S(1)}, bf16[32,1024]{1,0:T(8,128)(2,1)S(1)}, u32[]{:S(2)}, u32[]{:S(2)}) collective-permute-start(bf16[32,1024]{1,0:T(8,128)(2,1)S(1)} %get-tuple-element.6), channel_id=1, source_target_pairs={{0,2},{1,3},{2,0},{3,1},{4,6},{5,7},{6,4},{7,5},{8,10},{9,11},{10,... | collective-permute-start | bytes 196616 | tf_op jit(solution)/shard_map/ppermute | solution.py:202
  8.0 0.7 %collective-permute-done.2.refs_0_ = bf16[32,1024]{1,0:T(8,128)(2,1)S(1)} collective-permute-done((bf16[32,1024]{1,0:T(8,128)(2,1)S(1)}, bf16[32,1024]{1,0:T(8,128)(2,1)S(1)}, u32[]{:S(2)}, u32[]{:S(2)}) %collective-permute-start.2) | collective-permute-done | bytes 65568 | tf_op jit(solution)/shard_map/ppermute | solution.py:202
  8.7 2.5 %collective-permute-start.3 = (bf16[1,32,1024]{2,1,0:T(8,128)(2,1)S(1)}, bf16[1,32,1024]{2,1,0:T(8,128)(2,1)S(1)}, u32[]{:S(2)}, u32[]{:S(2)}) collective-permute-start(bf16[1,32,1024]{2,1,0:T(8,128)(2,1)S(1)} %shard_map.28), channel_id=1, source_target_pairs={{0,2},{1,3},{2,0},{3,1},{4,6},{5,7},{6,4},{7,5},{8,10},{9,11},{10,... | collective-permute-start | bytes 196616 | tf_op jit(solution)/shard_map/ppermute | solution.py:202
  11.3 0.0 collective-permute-done.4.refs_0_
  11.3 0.0 collective-permute-done.1.refs_0_
  11.3 1.6 %collective-permute-start.5 = (bf16[2,32,1024]{2,1,0:T(8,128)(2,1)S(1)}, bf16[2,32,1024]{2,1,0:T(8,128)(2,1)S(1)}, u32[]{:S(2)}, u32[]{:S(2)}) collective-permute-start(bf16[2,32,1024]{2,1,0:T(8,128)(2,1)S(1)} %shard_map.30), channel_id=1, source_target_pairs={{0,2},{1,3},{2,0},{3,1},{4,6},{5,7},{6,4},{7,5},{8,10},{9,11},{10,... | collective-permute-start | bytes 393224 | tf_op jit(solution)/shard_map/ppermute | solution.py:202
  12.9 0.0 collective-permute-done
  12.9 1.2 %collective-permute-done.3 = bf16[1,32,1024]{2,1,0:T(8,128)(2,1)S(1)} collective-permute-done((bf16[1,32,1024]{2,1,0:T(8,128)(2,1)S(1)}, bf16[1,32,1024]{2,1,0:T(8,128)(2,1)S(1)}, u32[]{:S(2)}, u32[]{:S(2)}) %collective-permute-start.3) | collective-permute-done | bytes 65568 | tf_op jit(solution)/shard_map/ppermute | solution.py:202
  14.1 0.1 collective-permute-start.6
  14.2 2.1 %collective-permute-done.5 = bf16[2,32,1024]{2,1,0:T(8,128)(2,1)S(1)} collective-permute-done((bf16[2,32,1024]{2,1,0:T(8,128)(2,1)S(1)}, bf16[2,32,1024]{2,1,0:T(8,128)(2,1)S(1)}, u32[]{:S(2)}, u32[]{:S(2)}) %collective-permute-start.5) | collective-permute-done | bytes 131104 | tf_op jit(solution)/shard_map/ppermute | solution.py:202
  16.4 0.1 collective-permute-start.7
  16.4 0.4 shard_map.32.half_ref
  16.8 0.0 collective-permute-done.6.other_ref
  16.8 0.5 %shard_map.33.wide_ref = f32[16,8,32,128]{3,2,1,0:T(8,128)S(1)} custom-call(f32[8,8,32,128]{3,2,1,0:T(8,128)S(1)} %shard_map.32.half_ref, bf16[6,32,1024]{2,1,0:T(8,128)(2,1)S(1)} %collective-permute-done.6.other_ref), custom_call_target="tpu_custom_call" | custom-call | flops 1000000 | bytes 10000 | tf_op jit(solution)/shard_map/pallas_call | solution.py:165
  17.3 0.5 %collective-permute-done.7.late_ref = bf16[2,32,1024]{2,1,0:T(8,128)(2,1)S(1)} collective-permute-done((bf16[2,32,1024]{2,1,0:T(8,128)(2,1)S(1)}, bf16[2,32,1024]{2,1,0:T(8,128)(2,1)S(1)}, u32[]{:S(2)}, u32[]{:S(2)}) %collective-permute-start.7) | collective-permute-done | bytes 131104 | tf_op jit(solution)/shard_map/ppermute | solution.py:202
  17.8 21.9 %shard_map.34 = f32[1024,16384]{1,0:T(8,128)} custom-call(f32[16,8,32,128]{3,2,1,0:T(8,128)S(1)} %shard_map.33.wide_ref, bf16[2,32,1024]{2,1,0:T(8,128)(2,1)S(1)} %collective-permute-done.7.late_ref), custom_call_target="tpu_custom_call" | custom-call | flops 1073741824 | bytes 67108864 | tf_op jit(solution)/shard_map/pallas_call | solution.py:178
  (10 shorter events, 0.1 us)
Async XLA Ops:
  0.9 7.9 %collective-permute-start.2 = (bf16[32,1024]{1,0:T(8,128)(2,1)S(1)}, bf16[32,1024]{1,0:T(8,128)(2,1)S(1)}, u32[]{:S(2)}, u32[]{:S(2)}) collective-permute-start(bf16[32,1024]{1,0:T(8,128)(2,1)S(1)} %get-tuple-element.6), channel_id=1, source_target_pairs={{0,8},{1,9},{2,10},{3,11},{4,12},{5,13},{6,14},{7,15},{8,0},{9,1},... | collective-permute-start | bytes 196616 | tf_op jit(solution)/shard_map/ppermute | solution.py:202
  5.0 6.3 %collective-permute-start.4 = (bf16[32,1024]{1,0:T(8,128)(2,1)S(1)}, bf16[32,1024]{1,0:T(8,128)(2,1)S(1)}, u32[]{:S(2)}, u32[]{:S(2)}) collective-permute-start(bf16[32,1024]{1,0:T(8,128)(2,1)S(1)} %get-tuple-element.6), channel_id=1, source_target_pairs={{0,12},{1,13},{2,14},{3,15},{4,8},{5,9},{6,10},{7,11},{8,4},{9,5},... | collective-permute-start | bytes 196616 | tf_op jit(solution)/shard_map/ppermute | solution.py:202
  6.3 5.0 %collective-permute-start.1 = (bf16[32,1024]{1,0:T(8,128)(2,1)S(1)}, bf16[32,1024]{1,0:T(8,128)(2,1)S(1)}, u32[]{:S(2)}, u32[]{:S(2)}) collective-permute-start(bf16[32,1024]{1,0:T(8,128)(2,1)S(1)} %get-tuple-element.6), channel_id=1, source_target_pairs={{0,4},{1,5},{2,6},{3,7},{4,0},{5,1},{6,2},{7,3},{8,12},{9,13},{10,... | collective-permute-start | bytes 196616 | tf_op jit(solution)/shard_map/ppermute | solution.py:202
  6.6 6.3 %collective-permute-start = (bf16[32,1024]{1,0:T(8,128)(2,1)S(1)}, bf16[32,1024]{1,0:T(8,128)(2,1)S(1)}, u32[]{:S(2)}, u32[]{:S(2)}) collective-permute-start(bf16[32,1024]{1,0:T(8,128)(2,1)S(1)} %get-tuple-element.6), channel_id=1, source_target_pairs={{0,2},{1,3},{2,0},{3,1},{4,6},{5,7},{6,4},{7,5},{8,10},{9,11},{10,... | collective-permute-start | bytes 196616 | tf_op jit(solution)/shard_map/ppermute | solution.py:202
  8.7 5.4 %collective-permute-start.3 = (bf16[1,32,1024]{2,1,0:T(8,128)(2,1)S(1)}, bf16[1,32,1024]{2,1,0:T(8,128)(2,1)S(1)}, u32[]{:S(2)}, u32[]{:S(2)}) collective-permute-start(bf16[1,32,1024]{2,1,0:T(8,128)(2,1)S(1)} %shard_map.28), channel_id=1, source_target_pairs={{0,2},{1,3},{2,0},{3,1},{4,6},{5,7},{6,4},{7,5},{8,10},{9,11},{10,... | collective-permute-start | bytes 196616 | tf_op jit(solution)/shard_map/ppermute | solution.py:202
  11.3 5.0 %collective-permute-start.5 = (bf16[2,32,1024]{2,1,0:T(8,128)(2,1)S(1)}, bf16[2,32,1024]{2,1,0:T(8,128)(2,1)S(1)}, u32[]{:S(2)}, u32[]{:S(2)}) collective-permute-start(bf16[2,32,1024]{2,1,0:T(8,128)(2,1)S(1)} %shard_map.30), channel_id=1, source_target_pairs={{0,2},{1,3},{2,0},{3,1},{4,6},{5,7},{6,4},{7,5},{8,10},{9,11},{10,... | collective-permute-start | bytes 393224 | tf_op jit(solution)/shard_map/ppermute | solution.py:202
  14.1 2.7 %collective-permute-start.6 = (bf16[6,32,1024]{2,1,0:T(8,128)(2,1)S(1)}, bf16[6,32,1024]{2,1,0:T(8,128)(2,1)S(1)}, u32[]{:S(2)}, u32[]{:S(2)}) collective-permute-start(bf16[6,32,1024]{2,1,0:T(8,128)(2,1)S(1)} %constant_dynamic-update-slice_fusion.early_ref), channel_id=1, source_target_pairs={{0,1},{1,0},{2,3},{3,2},{4,5},{5,4},{6,7},{7,6},{8,9},{9,8},{10,11... | collective-permute-start | bytes 1179656 | tf_op jit(solution)/shard_map/ppermute | solution.py:202
  16.4 1.4 %collective-permute-start.7 = (bf16[2,32,1024]{2,1,0:T(8,128)(2,1)S(1)}, bf16[2,32,1024]{2,1,0:T(8,128)(2,1)S(1)}, u32[]{:S(2)}, u32[]{:S(2)}) collective-permute-start(bf16[2,32,1024]{2,1,0:T(8,128)(2,1)S(1)} %shard_map.31.late_ref), channel_id=1, source_target_pairs={{0,1},{1,0},{2,3},{3,2},{4,5},{5,4},{6,7},{7,6},{8,9},{9,8},{10,11... | collective-permute-start | bytes 393224 | tf_op jit(solution)/shard_map/ppermute | solution.py:202

commit v6 on v5

--- a/solution.py
+++ b/solution.py
@@ -127,10 +127,11 @@
 
     @pl.loop(0, width // turn_width)
     def _(turn):
-        for i in range(turn_width // columns):
-            finish(turn * (turn_width // columns) + i, i * columns)
         for slot in range(BUFFERS):
             step = turn * BUFFERS + slot
+            for i in range(turn_width // columns):
+                if i * columns // CHUNK == slot:
+                    finish(turn * (turn_width // columns) + i, i * columns)
 
             @pl.when(turn > 0)
             def _():

time: 39.8 us -> 39.8 us (level)
  no operation moved by 1% of the time
where the time goes in v6:
time: 39.8 us; the launch traced here: 39.7 us
  Pallas kernels  22.7 us (57%)
  starting transfers between devices  11.4 us (29%)
  waiting for transfers between devices  4.53 us (11%)
  other arithmetic  0.87 us (2%)
    pallas_call x1, Pallas kernels, hessian_rows(): pl.pallas_call(functools.partial(hessian_kernel, ranks, late_at), in_spec...  21.9 us
    ppermute x8, starting transfers between devices, from_partner(): return lax.ppermute(x, 'tensor', [(i, i ^ k) for i in range(ranks)])  11.4 us
    ppermute x8, waiting for transfers between devices, from_partner(): return lax.ppermute(x, 'tensor', [(i, i ^ k) for i in range(ranks)])  4.53 us
    unnamed x1, other arithmetic  0.87 us
    pallas_call x2, Pallas kernels, in_vmem(): pl.pallas_call(kernel, in_specs=[pl.BlockSpec(memory_space=pltpu.VMEM)] *...  0.83 us
  transfers between devices with their start and end apart: 8, of which 4 were waited for; matrix products, arithmetic and copies ran while one was open for 0% of the time, Pallas kernels for 2%

profile of v6, /device:TPU:0, one launch (start us, length us, event | category | flops | bytes accessed | tf_op | source)
XLA Modules:
  0.0 39.7 jit_solution(13904291681785926584)
XLA Ops:
  0.0 0.9 %bitcast_dynamic-update-slice_fusion.3 = (bf16[6,32,1024]{2,1,0:T(8,128)(2,1)S(1)}, bf16[32,1024]{1,0:T(8,128)(2,1)S(1)}) fusion(bf16[32,1024]{1,0:T(8,128)(2,1)} %param.2, s32[1024]{0:T(1024)} %param.3), kind=kLoop, calls=%fused_computation.7 | loop fusion | flops 262143 | bytes 200704
  0.9 4.1 %collective-permute-start.2 = (bf16[32,1024]{1,0:T(8,128)(2,1)S(1)}, bf16[32,1024]{1,0:T(8,128)(2,1)S(1)}, u32[]{:S(2)}, u32[]{:S(2)}) collective-permute-start(bf16[32,1024]{1,0:T(8,128)(2,1)S(1)} %get-tuple-element.6), channel_id=1, source_target_pairs={{0,8},{1,9},{2,10},{3,11},{4,12},{5,13},{6,14},{7,15},{8,0},{9,1},... | collective-permute-start | bytes 196616 | tf_op jit(solution)/shard_map/ppermute | solution.py:203
  5.0 1.3 %collective-permute-start.4 = (bf16[32,1024]{1,0:T(8,128)(2,1)S(1)}, bf16[32,1024]{1,0:T(8,128)(2,1)S(1)}, u32[]{:S(2)}, u32[]{:S(2)}) collective-permute-start(bf16[32,1024]{1,0:T(8,128)(2,1)S(1)} %get-tuple-element.6), channel_id=1, source_target_pairs={{0,12},{1,13},{2,14},{3,15},{4,8},{5,9},{6,10},{7,11},{8,4},{9,5},... | collective-permute-start | bytes 196616 | tf_op jit(solution)/shard_map/ppermute | solution.py:203
  6.3 0.2 collective-permute-start.1
  6.6 1.5 %collective-permute-start = (bf16[32,1024]{1,0:T(8,128)(2,1)S(1)}, bf16[32,1024]{1,0:T(8,128)(2,1)S(1)}, u32[]{:S(2)}, u32[]{:S(2)}) collective-permute-start(bf16[32,1024]{1,0:T(8,128)(2,1)S(1)} %get-tuple-element.6), channel_id=1, source_target_pairs={{0,2},{1,3},{2,0},{3,1},{4,6},{5,7},{6,4},{7,5},{8,10},{9,11},{10,... | collective-permute-start | bytes 196616 | tf_op jit(solution)/shard_map/ppermute | solution.py:203
  8.0 0.7 %collective-permute-done.2.refs_0_ = bf16[32,1024]{1,0:T(8,128)(2,1)S(1)} collective-permute-done((bf16[32,1024]{1,0:T(8,128)(2,1)S(1)}, bf16[32,1024]{1,0:T(8,128)(2,1)S(1)}, u32[]{:S(2)}, u32[]{:S(2)}) %collective-permute-start.2) | collective-permute-done | bytes 65568 | tf_op jit(solution)/shard_map/ppermute | solution.py:203
  8.7 2.5 %collective-permute-start.3 = (bf16[1,32,1024]{2,1,0:T(8,128)(2,1)S(1)}, bf16[1,32,1024]{2,1,0:T(8,128)(2,1)S(1)}, u32[]{:S(2)}, u32[]{:S(2)}) collective-permute-start(bf16[1,32,1024]{2,1,0:T(8,128)(2,1)S(1)} %shard_map.28), channel_id=1, source_target_pairs={{0,2},{1,3},{2,0},{3,1},{4,6},{5,7},{6,4},{7,5},{8,10},{9,11},{10,... | collective-permute-start | bytes 196616 | tf_op jit(solution)/shard_map/ppermute | solution.py:203
  11.3 0.0 collective-permute-done.4.refs_0_
  11.3 0.0 collective-permute-done.1.refs_0_
  11.3 1.6 %collective-permute-start.5 = (bf16[2,32,1024]{2,1,0:T(8,128)(2,1)S(1)}, bf16[2,32,1024]{2,1,0:T(8,128)(2,1)S(1)}, u32[]{:S(2)}, u32[]{:S(2)}) collective-permute-start(bf16[2,32,1024]{2,1,0:T(8,128)(2,1)S(1)} %shard_map.30), channel_id=1, source_target_pairs={{0,2},{1,3},{2,0},{3,1},{4,6},{5,7},{6,4},{7,5},{8,10},{9,11},{10,... | collective-permute-start | bytes 393224 | tf_op jit(solution)/shard_map/ppermute | solution.py:203
  12.9 0.0 collective-permute-done
  12.9 1.2 %collective-permute-done.3 = bf16[1,32,1024]{2,1,0:T(8,128)(2,1)S(1)} collective-permute-done((bf16[1,32,1024]{2,1,0:T(8,128)(2,1)S(1)}, bf16[1,32,1024]{2,1,0:T(8,128)(2,1)S(1)}, u32[]{:S(2)}, u32[]{:S(2)}) %collective-permute-start.3) | collective-permute-done | bytes 65568 | tf_op jit(solution)/shard_map/ppermute | solution.py:203
  14.1 0.1 collective-permute-start.6
  14.2 2.1 %collective-permute-done.5 = bf16[2,32,1024]{2,1,0:T(8,128)(2,1)S(1)} collective-permute-done((bf16[2,32,1024]{2,1,0:T(8,128)(2,1)S(1)}, bf16[2,32,1024]{2,1,0:T(8,128)(2,1)S(1)}, u32[]{:S(2)}, u32[]{:S(2)}) %collective-permute-start.5) | collective-permute-done | bytes 131104 | tf_op jit(solution)/shard_map/ppermute | solution.py:203
  16.4 0.1 collective-permute-start.7
  16.4 0.4 shard_map.32.half_ref
  16.8 0.0 collective-permute-done.6.other_ref
  16.8 0.5 %shard_map.33.wide_ref = f32[16,8,32,128]{3,2,1,0:T(8,128)S(1)} custom-call(f32[8,8,32,128]{3,2,1,0:T(8,128)S(1)} %shard_map.32.half_ref, bf16[6,32,1024]{2,1,0:T(8,128)(2,1)S(1)} %collective-permute-done.6.other_ref), custom_call_target="tpu_custom_call" | custom-call | flops 1000000 | bytes 10000 | tf_op jit(solution)/shard_map/pallas_call | solution.py:166
  17.3 0.5 %collective-permute-done.7.late_ref = bf16[2,32,1024]{2,1,0:T(8,128)(2,1)S(1)} collective-permute-done((bf16[2,32,1024]{2,1,0:T(8,128)(2,1)S(1)}, bf16[2,32,1024]{2,1,0:T(8,128)(2,1)S(1)}, u32[]{:S(2)}, u32[]{:S(2)}) %collective-permute-start.7) | collective-permute-done | bytes 131104 | tf_op jit(solution)/shard_map/ppermute | solution.py:203
  17.8 21.9 %shard_map.34 = f32[1024,16384]{1,0:T(8,128)} custom-call(f32[16,8,32,128]{3,2,1,0:T(8,128)S(1)} %shard_map.33.wide_ref, bf16[2,32,1024]{2,1,0:T(8,128)(2,1)S(1)} %collective-permute-done.7.late_ref), custom_call_target="tpu_custom_call" | custom-call | flops 1073741824 | bytes 67108864 | tf_op jit(solution)/shard_map/pallas_call | solution.py:179
  (10 shorter events, 0.1 us)
Async XLA Ops:
  0.9 7.9 %collective-permute-start.2 = (bf16[32,1024]{1,0:T(8,128)(2,1)S(1)}, bf16[32,1024]{1,0:T(8,128)(2,1)S(1)}, u32[]{:S(2)}, u32[]{:S(2)}) collective-permute-start(bf16[32,1024]{1,0:T(8,128)(2,1)S(1)} %get-tuple-element.6), channel_id=1, source_target_pairs={{0,8},{1,9},{2,10},{3,11},{4,12},{5,13},{6,14},{7,15},{8,0},{9,1},... | collective-permute-start | bytes 196616 | tf_op jit(solution)/shard_map/ppermute | solution.py:203
  5.0 6.3 %collective-permute-start.4 = (bf16[32,1024]{1,0:T(8,128)(2,1)S(1)}, bf16[32,1024]{1,0:T(8,128)(2,1)S(1)}, u32[]{:S(2)}, u32[]{:S(2)}) collective-permute-start(bf16[32,1024]{1,0:T(8,128)(2,1)S(1)} %get-tuple-element.6), channel_id=1, source_target_pairs={{0,12},{1,13},{2,14},{3,15},{4,8},{5,9},{6,10},{7,11},{8,4},{9,5},... | collective-permute-start | bytes 196616 | tf_op jit(solution)/shard_map/ppermute | solution.py:203
  6.3 5.0 %collective-permute-start.1 = (bf16[32,1024]{1,0:T(8,128)(2,1)S(1)}, bf16[32,1024]{1,0:T(8,128)(2,1)S(1)}, u32[]{:S(2)}, u32[]{:S(2)}) collective-permute-start(bf16[32,1024]{1,0:T(8,128)(2,1)S(1)} %get-tuple-element.6), channel_id=1, source_target_pairs={{0,4},{1,5},{2,6},{3,7},{4,0},{5,1},{6,2},{7,3},{8,12},{9,13},{10,... | collective-permute-start | bytes 196616 | tf_op jit(solution)/shard_map/ppermute | solution.py:203
  6.6 6.3 %collective-permute-start = (bf16[32,1024]{1,0:T(8,128)(2,1)S(1)}, bf16[32,1024]{1,0:T(8,128)(2,1)S(1)}, u32[]{:S(2)}, u32[]{:S(2)}) collective-permute-start(bf16[32,1024]{1,0:T(8,128)(2,1)S(1)} %get-tuple-element.6), channel_id=1, source_target_pairs={{0,2},{1,3},{2,0},{3,1},{4,6},{5,7},{6,4},{7,5},{8,10},{9,11},{10,... | collective-permute-start | bytes 196616 | tf_op jit(solution)/shard_map/ppermute | solution.py:203
  8.7 5.4 %collective-permute-start.3 = (bf16[1,32,1024]{2,1,0:T(8,128)(2,1)S(1)}, bf16[1,32,1024]{2,1,0:T(8,128)(2,1)S(1)}, u32[]{:S(2)}, u32[]{:S(2)}) collective-permute-start(bf16[1,32,1024]{2,1,0:T(8,128)(2,1)S(1)} %shard_map.28), channel_id=1, source_target_pairs={{0,2},{1,3},{2,0},{3,1},{4,6},{5,7},{6,4},{7,5},{8,10},{9,11},{10,... | collective-permute-start | bytes 196616 | tf_op jit(solution)/shard_map/ppermute | solution.py:203
  11.3 5.0 %collective-permute-start.5 = (bf16[2,32,1024]{2,1,0:T(8,128)(2,1)S(1)}, bf16[2,32,1024]{2,1,0:T(8,128)(2,1)S(1)}, u32[]{:S(2)}, u32[]{:S(2)}) collective-permute-start(bf16[2,32,1024]{2,1,0:T(8,128)(2,1)S(1)} %shard_map.30), channel_id=1, source_target_pairs={{0,2},{1,3},{2,0},{3,1},{4,6},{5,7},{6,4},{7,5},{8,10},{9,11},{10,... | collective-permute-start | bytes 393224 | tf_op jit(solution)/shard_map/ppermute | solution.py:203
  14.1 2.7 %collective-permute-start.6 = (bf16[6,32,1024]{2,1,0:T(8,128)(2,1)S(1)}, bf16[6,32,1024]{2,1,0:T(8,128)(2,1)S(1)}, u32[]{:S(2)}, u32[]{:S(2)}) collective-permute-start(bf16[6,32,1024]{2,1,0:T(8,128)(2,1)S(1)} %constant_dynamic-update-slice_fusion.early_ref), channel_id=1, source_target_pairs={{0,1},{1,0},{2,3},{3,2},{4,5},{5,4},{6,7},{7,6},{8,9},{9,8},{10,11... | collective-permute-start | bytes 1179656 | tf_op jit(solution)/shard_map/ppermute | solution.py:203
  16.4 1.4 %collective-permute-start.7 = (bf16[2,32,1024]{2,1,0:T(8,128)(2,1)S(1)}, bf16[2,32,1024]{2,1,0:T(8,128)(2,1)S(1)}, u32[]{:S(2)}, u32[]{:S(2)}) collective-permute-start(bf16[2,32,1024]{2,1,0:T(8,128)(2,1)S(1)} %shard_map.31.late_ref), channel_id=1, source_target_pairs={{0,1},{1,0},{2,3},{3,2},{4,5},{5,4},{6,7},{7,6},{8,9},{9,8},{10,11... | collective-permute-start | bytes 393224 | tf_op jit(solution)/shard_map/ppermute | solution.py:203
